TPU v7x, 32 devices: a whole 2x2x4 slice. The times are simulated.
32 devices in a mesh: slab: 8 (over z, x), orb: 4 (over y, core).
Axes of the slice: x: 2, y: 2, z: 4, core: 2. Of those that a mesh axis runs over, the one named last changes fastest.
Arguments:
- orbitals: bfloat16 [2048, 128, 256], P(('slab', 'orb')), may hold values from -12 to 12
- region_start: int32 [2048], P(('slab', 'orb')), may hold values from 0 to 1023, as said below
- kin_cross: bfloat16 [256, 256], replicated, may hold values from -0.375 to 0.375
- potential: float32 [1024, 256], P(('slab', 'orb')), may hold values from 0.5 to 2
- pattern: int32 [32, 5], replicated, may hold values from 0 to 31, as said below
Outputs:
- gradient: bfloat16 [2048, 128, 256], P(('slab', 'orb'))
Inputs may be any that keep to these rules, and one draw needn't show every extreme that they name: `region_start`: region_start_i - (i // 256) * 128 lies in 0 to 127 and takes both ends within every slab's orbitals; regions continue periodically past the last grid column. `pattern`: row b lists 5 distinct blocks, b among them, all whose orbitals begin in slab b // 4 or the slab before or after it, taken periodically.
All inputs are finite; a program needn't handle non-finite values.
Results may differ from a plain program's by a relative error of at most 0.0085.
Values may be sent and summed in bfloat16 or wider, within the bound.
A program may use at most 128 MiB of HBM per device.

v0:
```python
import jax
import jax.numpy as jnp
from jax import lax
from jax.sharding import PartitionSpec as P

BLOCK = 64


def passed_along(array, axis, by):
    peers = lax.axis_size(axis)
    return lax.ppermute(array, axis, [(i, (i + by) % peers) for i in range(peers)])


def with_halo(array, sides, width):
    for axis, dim in sides:
        peers, length = (lax.axis_size(axis), array.shape[dim])
        up = [(i, (i + 1) % peers) for i in range(peers)]
        down = [(j, i) for i, j in up]
        last = lax.slice_in_dim(array, length - width, length, axis=dim)
        initial = lax.slice_in_dim(array, 0, width, axis=dim)
        before = lax.ppermute(last, axis, up)
        after = lax.ppermute(initial, axis, down)
        array = jnp.concatenate([before, array, after], axis=dim)
    return array


def kinetic_term(values, left_col, right_col, kin_cross):
    widen = values.astype(jnp.float32)
    before = jnp.concatenate([left_col, widen[:, :-1]], axis=1)
    after = jnp.concatenate([widen[:, 1:], right_col], axis=1)
    across = jnp.dot(
        values.reshape(-1, values.shape[2]), kin_cross, preferred_element_type=jnp.float32
    )
    across = across.reshape(widen.shape)
    return (0.5 * (2.0 * widen - before - after) + across).astype(jnp.bfloat16)


def window_rows(values, offset, length):

    def single(orb_row, begin_at):
        return lax.dynamic_slice_in_dim(orb_row, begin_at, length, 0)

    return jax.vmap(single)(values, offset)


def roll_rows(values, shift_by):
    length = values.shape[1]
    doubled = jnp.concatenate([values, values], axis=1)
    return window_rows(doubled, shift_by, length)


def per_device(orbitals, region_start, kin_cross, potential, pattern):
    held, length, cross = orbitals.shape
    orb_count = lax.axis_size("orb")
    slab_id = lax.axis_index("slab")
    orb_id = lax.axis_index("orb")
    per_slab = held * orb_count
    narrow = length // orb_count
    offset = region_start - slab_id * length
    edge = jnp.zeros((held, 1, cross), jnp.float32)
    kinetic = kinetic_term(orbitals, edge, edge, kin_cross)
    sources = [orbitals, kinetic]
    slab_offsets = lax.all_gather(region_start, "orb", axis=0, tiled=True) - slab_id * length
    columns = orb_id * narrow + jnp.arange(narrow, dtype=jnp.int32)
    in_own = (columns[None, :] >= slab_offsets[:, None])[None, :, :, None]
    rolled = jnp.stack([roll_rows(item, length - offset) for item in sources])
    pieces = lax.all_to_all(rolled, "orb", split_axis=2, concat_axis=1, tiled=True)
    own_half = jnp.where(in_own, pieces, jnp.zeros_like(pieces))
    ahead = jnp.where(in_own, jnp.zeros_like(pieces), pieces)
    moved = passed_along(ahead, "slab", 1)
    grid = jnp.concatenate([moved, own_half], axis=1)
    phi_grid = grid[0]
    kin_grid = grid[1]
    applied = (
        kin_grid.astype(jnp.float32) + potential[None] * phi_grid.astype(jnp.float32)
    ).astype(jnp.bfloat16)
    flat_phi = phi_grid.reshape(2 * per_slab, narrow * cross)
    flat_app = applied.reshape(2 * per_slab, narrow * cross)
    volume = 1.0 / (length * cross)
    contract_rows = (((1,), (1,)), ((), ()))
    contract_cols = (((0,), (0,)), ((), ()))
    intersection = (
        lax.dot_general(flat_phi, flat_phi, contract_rows, preferred_element_type=jnp.float32)
        * volume
    )
    hamilton = (
        lax.dot_general(flat_phi, flat_app, contract_rows, preferred_element_type=jnp.float32)
        * volume
    )
    intersection, hamilton = lax.psum((intersection, hamilton), "orb")
    corners = jnp.stack(
        [
            jnp.stack([intersection[:per_slab, :per_slab], hamilton[:per_slab, :per_slab]]),
            jnp.stack([intersection[per_slab:, per_slab:], hamilton[per_slab:, per_slab:]]),
        ]
    )
    rims = with_halo(corners, (("slab", 0),), 1)
    zero_pair = jnp.zeros((per_slab, per_slab), jnp.float32)
    intersection = intersection + jnp.block([[rims[0, 0], zero_pair], [zero_pair, rims[3, 0]]])
    hamilton = hamilton + jnp.block([[rims[0, 1], zero_pair], [zero_pair, rims[3, 1]]])
    blk_slab = per_slab // BLOCK
    nblk = pattern.shape[0]
    block_ids = ((slab_id - 1) * blk_slab + jnp.arange(2 * blk_slab, dtype=jnp.int32)) % nblk
    rows_listed = jnp.take(pattern, block_ids, axis=0)
    sub_cover = jnp.any(rows_listed[:, :, None] == block_ids[None, None, :], axis=1).astype(
        jnp.float32
    )
    orb_cover = jnp.repeat(jnp.repeat(sub_cover, BLOCK, axis=0), BLOCK, axis=1)
    masked_intersection = (intersection * orb_cover).astype(jnp.bfloat16)
    masked_hamilton = (hamilton * orb_cover).astype(jnp.bfloat16)
    scale = 1.0 / (pattern.shape[1] * BLOCK)
    first = lax.dot_general(
        masked_intersection, flat_app, contract_cols, preferred_element_type=jnp.float32
    )
    second = lax.dot_general(
        masked_hamilton, flat_phi, contract_cols, preferred_element_type=jnp.float32
    )
    grad_grid = ((first - second) * scale).astype(jnp.bfloat16).reshape(2 * per_slab, narrow, cross)
    returned = passed_along(grad_grid[:per_slab], "slab", -1)
    combined = jnp.where(in_own[0], grad_grid[per_slab:], returned)
    owned = lax.all_to_all(combined, "orb", split_axis=0, concat_axis=1, tiled=True)
    return roll_rows(owned, offset)


def solution(mesh):
    placed = (
        P(("slab", "orb"), None, None),
        P(("slab", "orb")),
        P(),
        P(("slab", "orb"), None),
        P(),
    )
    return jax.shard_map(
        per_device,
        mesh=mesh,
        in_specs=placed,
        out_specs=P(("slab", "orb"), None, None),
        check_vma=False,
    )
```

profile of v0, /device:TPU:0, one launch (start us, length us, event | category | flops | bytes accessed | tf_op | source)
XLA Modules:
  0.0 724.4 jit_solution(5803490538275493629)
XLA Ops:
  13.3 7.6 %fusion.58 = (f32[64,127,256]{2,1,0:T(8,128)}, f32[64,127,256]{2,1,0:T(8,128)}) fusion(bf16[64,128,256]{2,1,0:T(8,128)(2,1)S(1)} %copy-done.2), kind=kLoop, calls=%fused_computation.93 | loop fusion | bytes 33292288 | tf_op jit(solution)/shard_map/slice | solution.py:29
  20.9 7.4 %pad_maximum_fusion.1 = bf16[64,256,256]{2,0,1:T(8,128)(2,1)} fusion(bf16[64,128,256]{2,0,1:T(8,128)(2,1)} %copy.40), kind=kLoop, calls=%fused_computation.15 | loop fusion | flops 4194304 | bytes 12582912 | tf_op jit(solution)/shard_map/concatenate | solution.py:48
  28.3 11.9 %add_convert_fusion.1 = bf16[64,128,256]{2,1,0:T(8,128)(2,1)} fusion(f32[64,127,256]{2,1,0:T(8,128)} %get-tuple-element.14, f32[64,127,256]{2,1,0:T(8,128)} %get-tuple-element.13, bf16[64,128,256]{2,1,0:T(8,128)(2,1)} %param.5, bf16[256,256]{1,0:T(8,128)(2,1)S(1)} %copy-done), kind=kOutput, calls=%fused_computation.25 | convolution fusion | flops 1088421888 | bytes 25165824 | tf_op jit(solution)/shard_map/dot_general | solution.py:31
  40.3 7.7 %pad_maximum_fusion.2 = bf16[64,256,256]{2,1,0:T(8,128)(2,1)} fusion(bf16[64,128,256]{2,1,0:T(8,128)(2,1)} %add_convert_fusion.1), kind=kLoop, calls=%fused_computation.16 | loop fusion | flops 16777216 | bytes 12582912 | tf_op jit(solution)/shard_map/concatenate | solution.py:48
  48.0 11.4 %copy.42 = bf16[64,256,256]{2,0,1:T(8,128)(2,1)} copy(bf16[64,256,256]{2,1,0:T(8,128)(2,1)} %pad_maximum_fusion.2) | data formatting | bytes 16777216 | tf_op jit(solution)/shard_map/concatenate | solution.py:48
  59.4 13.2 %gather_fusion.1 = bf16[64,128,256]{2,0,1:T(8,128)(2,1)} fusion(bf16[64,256,256]{2,0,1:T(8,128)(2,1)} %pad_maximum_fusion.1, s32[64]{0:T(128)S(1)} %get-tuple-element.24), kind=kCustom, calls=%fused_computation.1 | custom fusion | bytes 8389376 | tf_op jit(solution)/shard_map/vmap()/gather | solution.py:41
  72.6 12.8 %gather_fusion.2 = bf16[64,128,256]{2,0,1:T(8,128)(2,1)} fusion(bf16[64,256,256]{2,0,1:T(8,128)(2,1)} %copy.42, s32[64]{0:T(128)S(1)} %get-tuple-element.24), kind=kCustom, calls=%fused_computation.2 | custom fusion | bytes 8389376 | tf_op jit(solution)/shard_map/vmap()/gather | solution.py:41
  85.4 7.5 %pad_maximum_fusion.3 = bf16[2,64,128,256]{3,1,2,0:T(8,128)(2,1)} fusion(bf16[1,64,128,256]{3,1,2,0:T(8,128)(2,1)} %bitcast.105, bf16[1,64,128,256]{3,1,2,0:T(8,128)(2,1)} %bitcast.104), kind=kLoop, calls=%fused_computation.17 | loop fusion | flops 4194304 | bytes 16777216 | tf_op jit(solution)/shard_map/stack | solution.py:66
  92.9 8.3 %copy.43 = bf16[2,64,128,256]{3,1,0,2:T(8,128)(2,1)} copy(bf16[2,64,128,256]{3,1,2,0:T(8,128)(2,1)} %pad_maximum_fusion.3) | data formatting | bytes 16777216 | tf_op jit(solution)/shard_map/stack | solution.py:66
  108.5 92.3 %all-reduce.8 = s32[256]{0:T(256)S(1)} all-reduce(s32[256]{0:T(256)S(1)} %dynamic-update-slice), channel_id=1, replica_groups=mesh['slab'=8,'orb'=4] {'orb'}, use_global_device_ids=true, to_apply=%add.8 | all-reduce | flops 256 | bytes 2048
  200.9 8.3 %copy.44 = bf16[2,64,4,32,256]{4,1,2,3,0:T(8,128)(2,1)} copy(bf16[2,64,4,32,256]{4,1,0,3,2:T(8,128)(2,1)} %bitcast.6) | data formatting | bytes 16777216 | tf_op jit(solution)/shard_map/all_to_all | solution.py:67
  216.2 183.3 %collective-permute-done = bf16[2,256,32,256]{3,1,2,0:T(8,128)(2,1)S(1)} collective-permute-done((bf16[2,256,32,256]{3,1,2,0:T(8,128)(2,1)S(1)}, bf16[2,256,32,256]{3,1,2,0:T(8,128)(2,1)S(1)}, u32[]{:S(2)}, u32[]{:S(2)}) %collective-permute-start) | collective-permute-done | bytes 8388640 | tf_op jit(solution)/shard_map/ppermute | solution.py:11
  399.5 7.5 %fusion.4 = (bf16[1,512,32,256]{3,1,2,0:T(8,128)(2,1)S(1)}, f32[1,512,32,256]{3,1,2,0:T(8,128)}) fusion(bf16[2,256,32,256]{3,1,2,0:T(8,128)(2,1)S(1)} %collective-permute-done, bf16[2,256,32,256]{3,1,2,0:T(8,128)(2,1)S(1)} %get-tuple-element.10), kind=kLoop, calls=%fused_computation.12 | loop fusion | flops 33554432 | bytes 41943040 | tf_op jit(solution)/shard_map/concatenate | solution.py:71
  416.6 13.7 %fusion.21 = f32[512,512]{1,0:T(8,128)} fusion(bf16[1,512,32,256]{3,1,2,0:T(8,128)(2,1)} %copy-done.3, f32[32,256]{1,0:T(8,128)S(1)} %copy-done.7, bf16[2,256,32,256]{3,1,2,0:T(8,128)(2,1)} %copy-done.4, bf16[2,256,32,256]{3,1,2,0:T(8,128)(2,1)} %copy-done.5), kind=kOutput, calls=%fused_computation.30 | convolution fusion | flops 4328783872 | bytes 26247168 | tf_op jit(solution)/shard_map/dot_general | solution.py:87
  431.9 12.0 %copy.50 = bf16[1,512,32,256]{1,3,2,0:T(8,128)(2,1)} copy(bf16[1,512,32,256]{3,1,2,0:T(8,128)(2,1)} %copy-done.3) | data formatting | bytes 16777216 | tf_op jit(solution)/shard_map/slice | solution.py:72
  443.9 17.6 %copy.49 = f32[1,512,32,256]{1,3,2,0:T(8,128)} copy(f32[1,512,32,256]{3,1,2,0:T(8,128)} %get-tuple-element.8) | data formatting | bytes 33554432 | tf_op jit(solution)/shard_map/convert_element_type | solution.py:75
  461.5 18.1 %all-reduce.12.cloned.1.call-done = (f32[512,512]{1,0:T(8,128)}, f32[512,512]{1,0:T(8,128)}) async-done(((f32[512,512]{1,0:T(8,128)}, f32[512,512]{1,0:T(8,128)}), (f32[512,512]{1,0:T(8,128)}, f32[512,512]{1,0:T(8,128)})) %all-reduce.12.cloned.1.call-update) | async-done | bytes 2097168 | tf_op jit(solution)/shard_map/psum | solution.py:90
  485.2 9.3 %fusion = bf16[512,8192]{0,1:T(8,128)(2,1)S(1)} fusion(f32[1,512,32,256]{1,3,2,0:T(8,128)} %copy.49, f32[8192]{0:T(1024)S(1)} %bitcast.107, bf16[1,512,32,256]{1,3,2,0:T(8,128)(2,1)} %copy.50), kind=kLoop, calls=%fused_computation.7 | loop fusion | flops 16777216 | bytes 33587200 | tf_op jit(solution)/shard_map/convert_element_type | solution.py:76
  494.5 11.2 %collective-permute-done.2 = f32[1,2,256,256]{3,2,1,0:T(8,128)S(1)} collective-permute-done((f32[1,2,256,256]{3,2,1,0:T(8,128)S(1)}, f32[1,2,256,256]{3,2,1,0:T(8,128)S(1)}, u32[]{:S(2)}, u32[]{:S(2)}) %collective-permute-start.2) | collective-permute-done | bytes 524320 | tf_op jit(solution)/shard_map/ppermute | solution.py:22
  506.5 9.6 %fusion.32 = f32[512,8192]{1,0:T(8,128)} fusion(bf16[512,8192]{0,1:T(8,128)(2,1)S(1)} %fusion, f32[512,512]{1,0:T(8,128)S(1)} %copy.48, f32[512,512]{1,0:T(8,128)} %get-tuple-element.5, f32[256,256]{1,0:T(8,128)S(1)} %get-tuple-element.22, f32[256,256]{1,0:T(8,128)} %get-tuple-element.20), kind=kOutput, calls=%fused_computation.41 | convolution fusion | flops 4297064448 | bytes 27787264 | tf_op jit(solution)/shard_map/dot_general | solution.py:112
  516.1 12.8 %multiply_convert_fusion = bf16[512,8192]{1,0:T(8,128)(2,1)} fusion(f32[512,8192]{1,0:T(8,128)} %fusion.32, bf16[512,8192]{0,1:T(8,128)(2,1)} %bitcast.99, f32[512,512]{1,0:T(8,128)S(1)} %copy.48, f32[512,512]{1,0:T(8,128)S(1)} %copy-done.6, f32[256,256]{1,0:T(8,128)S(1)} %get-tuple-element.21, f32[256,256]{1,0:T(8,128)S(1)} %get-tuple-element.19), kind=kOutput, calls=%fused_computation.8 | convolution fusion | flops 4309647360 | bytes 36175872 | tf_op jit(solution)/shard_map/dot_general | solution.py:115
  545.6 85.2 %collective-permute-done.3 = bf16[256,32,256]{2,1,0:T(8,128)(2,1)} collective-permute-done((bf16[256,32,256]{2,1,0:T(8,128)(2,1)}, bf16[256,32,256]{2,1,0:T(8,128)(2,1)}, u32[]{:S(2)}, u32[]{:S(2)}) %collective-permute-start.3) | collective-permute-done | bytes 4194336 | tf_op jit(solution)/shard_map/ppermute | solution.py:11
  635.1 50.7 %all_to_all.36 = bf16[256,32,256]{2,1,0:T(8,128)(2,1)S(1)} all-to-all(bf16[256,32,256]{2,1,0:T(8,128)(2,1)S(1)} %bitcast_select_fusion.2), channel_id=1, replica_groups=mesh['slab'=8,'orb'=4] {'orb'}, dimensions={0} | all-to-all | bytes 8388608 | tf_op jit(solution)/shard_map/all_to_all | solution.py:121
  697.8 12.8 %gather_fusion.3 = bf16[64,128,256]{2,0,1:T(8,128)(2,1)} fusion(bf16[64,256,256]{2,0,1:T(8,128)(2,1)} %pad_maximum_fusion.4, s32[64]{0:T(128)S(1)} %get-tuple-element.23), kind=kCustom, calls=%fused_computation.3 | custom fusion | bytes 8389376 | tf_op jit(solution)/shard_map/vmap()/gather | solution.py:41
  (70 shorter events, 77.7 us)
Async XLA Ops:
  6.5 21.8 %copy-start = (bf16[256,256]{1,0:T(8,128)(2,1)S(1)}, bf16[256,256]{1,0:T(8,128)(2,1)}, u32[]{:S(2)}) copy-start(bf16[256,256]{1,0:T(8,128)(2,1)} %param.7) | copy-start | bytes 393220
  6.5 6.7 copy-start.2
  48.0 11.4 %copy-start.9 = (s32[64]{0:T(128)S(1)}, s32[64]{0:T(128)}, u32[]{:S(2)}) copy-start(s32[64]{0:T(128)} %param.6) | copy-start | bytes 772
  101.1 5.8 copy-start.10
  101.1 99.7 %all-to-all-start = ((bf16[2,64,128,256]{3,1,0,2:T(8,128)(2,1)}), bf16[2,64,128,256]{3,1,0,2:T(8,128)(2,1)}, u32[]{:S(2)}, u32[]{:S(2)}) async-start(bf16[2,64,128,256]{3,1,0,2:T(8,128)(2,1)} %copy.43), calls=%async_computation | async-start | bytes 16777216 | tf_op jit(solution)/shard_map/all_to_all | solution.py:67
  106.9 372.6 %all-reduce.12.cloned.1.call-start = ((), (), s32[]{:S(2)}) async-start(), calls=%async_computation.2 | async-start | bytes 4194304 | tf_op jit(solution)/shard_map/psum | solution.py:90
  213.8 193.2 %copy-start.4 = (bf16[2,256,32,256]{3,1,2,0:T(8,128)(2,1)}, bf16[2,256,32,256]{3,1,2,0:T(8,128)(2,1)S(1)}, u32[]{:S(2)}) copy-start(bf16[2,256,32,256]{3,1,2,0:T(8,128)(2,1)S(1)} %get-tuple-element.10) | copy-start | bytes 25165828
  213.9 185.7 %collective-permute-start = (bf16[2,256,32,256]{3,1,2,0:T(8,128)(2,1)S(1)}, bf16[2,256,32,256]{3,1,2,0:T(8,128)(2,1)S(1)}, u32[]{:S(2)}, u32[]{:S(2)}) collective-permute-start(bf16[2,256,32,256]{3,1,2,0:T(8,128)(2,1)S(1)} %get-tuple-element.9), channel_id=1, source_target_pairs={{0,4},{4,8},{8,12},{12,16},{16,20},{20,24},{24,28},{28,0},{1,5},{5... | collective-permute-start | bytes 25165832 | tf_op jit(solution)/shard_map/ppermute | solution.py:11
  399.5 8.3 %copy-start.5 = (bf16[2,256,32,256]{3,1,2,0:T(8,128)(2,1)}, bf16[2,256,32,256]{3,1,2,0:T(8,128)(2,1)S(1)}, u32[]{:S(2)}) copy-start(bf16[2,256,32,256]{3,1,2,0:T(8,128)(2,1)S(1)} %collective-permute-done) | copy-start | bytes 25165828
  407.8 3.2 copy-start.3
  411.1 5.5 copy-start.7
  416.5 13.7 %copy-start.8 = (s32[32,5]{0,1:T(8,128)S(1)}, s32[32,5]{0,1:T(8,128)}, u32[]{:S(2)}) copy-start(s32[32,5]{0,1:T(8,128)} %param.9) | copy-start | bytes 1924
  480.9 24.9 %collective-permute-start.2 = (f32[1,2,256,256]{3,2,1,0:T(8,128)S(1)}, f32[1,2,256,256]{3,2,1,0:T(8,128)S(1)}, u32[]{:S(2)}, u32[]{:S(2)}) collective-permute-start(f32[1,2,256,256]{3,2,1,0:T(8,128)S(1)} %maximum_bitcast_fusion.1), channel_id=1, source_target_pairs={{4,0},{8,4},{12,8},{16,12},{20,16},{24,20},{28,24},{0,28},{5,1},{9... | collective-permute-start | bytes 1572872 | tf_op jit(solution)/shard_map/ppermute | solution.py:22
  485.2 20.6 %collective-permute-start.1 = (f32[1,2,256,256]{3,2,1,0:T(8,128)S(1)}, f32[1,2,256,256]{3,2,1,0:T(8,128)S(1)}, u32[]{:S(2)}, u32[]{:S(2)}) collective-permute-start(f32[1,2,256,256]{3,2,1,0:T(8,128)S(1)} %maximum_bitcast_fusion), channel_id=1, source_target_pairs={{0,4},{4,8},{8,12},{12,16},{16,20},{20,24},{24,28},{28,0},{1,5},{5... | collective-permute-start | bytes 1572872 | tf_op jit(solution)/shard_map/ppermute | solution.py:21
  506.5 9.6 %copy-start.6 = (f32[512,512]{1,0:T(8,128)S(1)}, f32[512,512]{1,0:T(8,128)}, u32[]{:S(2)}) copy-start(f32[512,512]{1,0:T(8,128)} %get-tuple-element.6) | copy-start | bytes 3145732
  537.3 93.4 %collective-permute-start.3 = (bf16[256,32,256]{2,1,0:T(8,128)(2,1)}, bf16[256,32,256]{2,1,0:T(8,128)(2,1)}, u32[]{:S(2)}, u32[]{:S(2)}) collective-permute-start(bf16[256,32,256]{2,1,0:T(8,128)(2,1)} %bitcast.40), channel_id=1, source_target_pairs={{0,28},{4,0},{8,4},{12,8},{16,12},{20,16},{24,20},{28,24},{1,29},{... | collective-permute-start | bytes 12582920 | tf_op jit(solution)/shard_map/ppermute | solution.py:11
  697.8 19.4 %copy-start.1 = (bf16[256,256]{1,0:T(8,128)(2,1)S(1)}, bf16[256,256]{1,0:T(8,128)(2,1)}, u32[]{:S(2)}) copy-start(bf16[256,256]{1,0:T(8,128)(2,1)} %param.7) | copy-start | bytes 393220
Sparse Core Ops, SparseCore 0:
  430.4 49.1 all-reduce.11
where the time goes:
time: 730 us; the launch traced here: 724 us
  waiting for transfers between devices  298 us (41%)
  blocking collectives  143 us (20%)
  local copies, waits for them, and re-layouts  142 us (19%)
  other arithmetic  56.3 us (8%)
  matrix products  53.4 us (7%)
  starting transfers between devices  17.1 us (2%)
  between operations  14.7 us (2%)
    ppermute x2, waiting for transfers between devices, passed_along(): lax.ppermute(array, axis, [(i, (i + by) % peers) for i in range(peers)])  268 us
    unnamed x1, blocking collectives  92.3 us
    all_to_all x1, blocking collectives, per_device(): lax.all_to_all(combined, 'orb', split_axis=0, concat_axis=1, tiled=True)  50.7 us
    gather x4, local copies, waits for them, and re-layouts, single(): return lax.dynamic_slice_in_dim(orb_row, begin_at, length, 0)  45.4 us
    concatenate x3, other arithmetic, roll_rows(): doubled = jnp.concatenate([values, values], axis=1)  22.6 us
    unnamed x30, local copies, waits for them, and re-layouts  18.6 us
    psum x1, waiting for transfers between devices, per_device(): intersection, hamilton = lax.psum((intersection, hamilton), 'orb')  18.1 us
    convert_element_type x1, local copies, waits for them, and re-layouts, per_device(): kin_grid.astype(jnp.float32)  17.6 us
  transfers between devices with their start and end apart: 6, of which 4 were waited for; matrix products, arithmetic and copies ran while one was open for 6% of the time, Pallas kernels for 0%

commit v1 on v0

v1 whole, which is shorter than its diff:
```python
import functools

import jax
import jax.numpy as jnp
from jax import lax
from jax.experimental import pallas as pl
from jax.experimental.pallas import tpu as pltpu
from jax.sharding import PartitionSpec as P

BLOCK = 64
CHUNKS = 2
VMEM = 50 * 1024 * 1024
F32 = jnp.float32
BF16 = jnp.bfloat16
ROWS = (((1,), (1,)), ((), ()))
MAJOR = (((1,), (0,)), ((), ()))


def column(refs, at):
    parts = [ref[:, at].reshape(-1, ref.shape[3]) for ref in refs]
    return jnp.concatenate(parts, axis=0)


def kinetic_of(refs, col, place, filt, off, length):
    phi = column(refs, col + 1)
    before = column(refs, col).astype(F32)
    after = column(refs, col + 2).astype(F32)
    zero = jnp.zeros_like(before)
    before = jnp.where(off == place, zero, before)
    last = jnp.where(off == 0.0, F32(length), off) - 1.0
    after = jnp.where(last == place, zero, after)
    wide = phi.astype(F32)
    across = lax.dot_general(phi, filt, MAJOR, preferred_element_type=F32)
    kin = (0.5 * (2.0 * wide - before - after) + across).astype(BF16)
    return wide, kin.astype(F32)


def own_kernel(chunks, length, *refs):
    parts = refs[:chunks]
    off_ref, base_ref, filt_ref, pot_ref, right_ref, sums_ref = refs[chunks:]
    col = pl.program_id(0)
    place = base_ref[0] + col.astype(F32)
    off = off_ref[...]
    wide, kin = kinetic_of(parts, col, place, filt_ref[...], off, length)
    count = wide.shape[0]
    own = off <= place
    zero = jnp.zeros_like(wide)

    @pl.when(col == 0)
    def _():
        sums_ref[...] = jnp.zeros_like(sums_ref)

    total = sums_ref[...]
    for side in range(2):
        app = kin + pot_ref[side, pl.ds(col, 1), :] * wide
        keep = own if side == 0 else jnp.logical_not(own)
        phi_side = jnp.where(keep, wide, zero).astype(BF16)
        app_side = jnp.where(keep, app, zero).astype(BF16)
        right_ref[0, side, :count] = phi_side
        right_ref[0, side, count:] = app_side
        both = jnp.concatenate([phi_side, app_side], axis=0)
        total += lax.dot_general(both, phi_side, ROWS, preferred_element_type=F32)
    sums_ref[...] = total


def other_kernel(chunks, length, *refs):
    parts = refs[:chunks]
    off_ref, base_ref, side_ref, filt_ref, pot_ref, right_ref, left_ref, sums_ref = refs[chunks:]
    col = pl.program_id(0)
    place = base_ref[0] + col.astype(F32)
    off = off_ref[...]
    wide, kin = kinetic_of(parts, col, place, filt_ref[...], off, length)
    count = wide.shape[0]
    side = side_ref[0]
    sign = jnp.where(side == 0, F32(-1.0), F32(1.0))
    keep = (place + 0.5 - off) * sign > 0.0
    zero = jnp.zeros_like(wide)
    app = kin + pot_ref[side, pl.ds(col, 1), :] * wide
    phi_side = jnp.where(keep, wide, zero).astype(BF16)
    app_side = jnp.where(keep, app, zero).astype(BF16)
    left_ref[0, :count] = phi_side
    left_ref[0, count:] = app_side

    @pl.when(col == 0)
    def _():
        sums_ref[...] = jnp.zeros_like(sums_ref)

    sums_ref[...] += lax.dot_general(
        right_ref[0, side], phi_side, ROWS, preferred_element_type=F32
    )


def gradient_kernel(chunks, scale, *refs):
    off_ref, base_ref, side_ref, weight_ref, right_ref, one_ref, two_ref, out_ref = refs
    col = pl.program_id(0)
    place = base_ref[0] + col.astype(F32)
    off = off_ref[...]
    sign = jnp.where(side_ref[0] == 0, F32(1.0), F32(-1.0))
    own = off <= place
    with_one = (place + 0.5 - off) * sign > 0.0

    def product(which, block):
        return lax.dot_general(weight_ref[which], block, MAJOR, preferred_element_type=F32)

    near = jnp.where(own, product(0, right_ref[0, 0]), product(0, right_ref[0, 1]))
    far = jnp.where(with_one, product(1, one_ref[0]), product(2, two_ref[0]))
    grad = ((near + far) * scale).astype(BF16)
    peers, per = out_ref.shape[0], out_ref.shape[2] // chunks
    for chunk in range(chunks):
        for peer in range(peers):
            at = (chunk * peers + peer) * per
            out_ref[peer, 0, chunk * per:(chunk + 1) * per, :] = grad[at:at + per]


def whole(array):
    return pl.BlockSpec(array.shape, lambda col: (0,) * array.ndim)


def per_col(shape, lead=0):
    def index(col):
        return tuple(col if at == lead else 0 for at in range(len(shape)))

    block = tuple(1 if at == lead else size for at, size in enumerate(shape))
    return pl.BlockSpec(block, index)


SMEM = pl.BlockSpec(memory_space=pltpu.SMEM)
PARAMS = pltpu.CompilerParams(vmem_limit_bytes=VMEM)


def window_rows(values, offset, length):
    def single(orb_row, begin_at):
        return lax.dynamic_slice_in_dim(orb_row, begin_at, length, 0)

    return jax.vmap(single)(values, offset)


def per_device(orbitals, region_start, kin_cross, potential, pattern):
    held, length, cross = orbitals.shape
    peers = lax.axis_size("orb")
    slabs = lax.axis_size("slab")
    slab_id = lax.axis_index("slab")
    orb_id = lax.axis_index("orb")
    per_slab = held * peers
    narrow = length // peers
    per = held // CHUNKS
    offset = region_start - slab_id * length

    starts = lax.all_gather(region_start, ("slab", "orb"), axis=0, tiled=True)
    starts = starts.reshape(slabs, per_slab)
    ids = jnp.arange(per_slab, dtype=jnp.int32).reshape(peers, CHUNKS, per)
    ids = ids.transpose(1, 0, 2).reshape(per_slab)
    odd = slab_id % 2
    first = slab_id + 1 - 2 * odd
    second = lax.rem(slab_id - 1 + 2 * odd + slabs, slabs)
    first_side = (1 - odd).astype(jnp.int32)
    groups = [slab_id, first, second]
    offs = []
    for group in groups:
        row = lax.dynamic_index_in_dim(starts, group, 0, keepdims=False) - group * length
        row = row.reshape(peers, CHUNKS, per).transpose(1, 0, 2).reshape(per_slab, 1)
        offs.append(jnp.broadcast_to(row.astype(F32), (per_slab, cross)))
    base = (orb_id * narrow).astype(F32).reshape(1)
    pot_next = lax.ppermute(potential, "slab", [(i, (i - 1) % slabs) for i in range(slabs)])
    pots = jnp.stack([potential, pot_next])

    swap = [(i, i ^ 1) for i in range(slabs)]
    onward = [(i, (i + 2 - 4 * (i % 2)) % slabs) for i in range(slabs)]
    own_parts, one_parts, two_parts = [], [], []
    for chunk in range(CHUNKS):
        rows = slice(chunk * per, (chunk + 1) * per)
        values = orbitals[rows]
        around = jnp.concatenate([values, values, values[:, :2]], axis=1)
        rolled = window_rows(around, length - 1 - offset[rows], length + 2)
        cut = jnp.stack([rolled[:, d * narrow:(d + 1) * narrow + 2] for d in range(peers)])
        cut = cut.transpose(0, 2, 1, 3)
        own_parts.append(lax.all_to_all(cut, "orb", split_axis=0, concat_axis=0, tiled=True))
    for part in own_parts:
        one_parts.append(lax.ppermute(part, "slab", swap))
    for part in one_parts:
        two_parts.append(lax.ppermute(part, "slab", onward))

    right_shape = (narrow, 2, 2 * per_slab, cross)
    left_shape = (narrow, 2 * per_slab, cross)
    sums_shape = (2 * per_slab, per_slab)
    sums_spec = pl.BlockSpec(sums_shape, lambda col: (0, 0))
    product = 2 * per_slab * per_slab * cross * narrow
    right, own_sums = pl.pallas_call(
        functools.partial(own_kernel, CHUNKS, length),
        grid=(narrow,),
        in_specs=[whole(p) for p in own_parts]
        + [whole(offs[0]), SMEM, whole(kin_cross), whole(pots)],
        out_specs=[per_col(right_shape), sums_spec],
        out_shape=[
            jax.ShapeDtypeStruct(right_shape, BF16),
            jax.ShapeDtypeStruct(sums_shape, F32),
        ],
        compiler_params=PARAMS,
        cost_estimate=pl.CostEstimate(
            flops=5 * product, bytes_accessed=22 * 2**20, transcendentals=0
        ),
    )(*own_parts, offs[0], base, kin_cross, pots)

    def other(parts, off, side):
        return pl.pallas_call(
            functools.partial(other_kernel, CHUNKS, length),
            grid=(narrow,),
            in_specs=[whole(p) for p in parts]
            + [whole(off), SMEM, SMEM, whole(kin_cross), whole(pots), per_col(right_shape)],
            out_specs=[per_col(left_shape), sums_spec],
            out_shape=[
                jax.ShapeDtypeStruct(left_shape, BF16),
                jax.ShapeDtypeStruct(sums_shape, F32),
            ],
            compiler_params=PARAMS,
            cost_estimate=pl.CostEstimate(
                flops=3 * product, bytes_accessed=30 * 2**20, transcendentals=0
            ),
        )(*parts, off, base, side.reshape(1), kin_cross, pots, right)

    one_left, one_sums = other(one_parts, offs[1], first_side)
    sums_a = lax.psum(jnp.stack([own_sums, one_sums]), "orb")
    two_left, two_sums = other(two_parts, offs[2], 1 - first_side)
    sums_b = lax.psum(two_sums, "orb")

    blk_slab = per_slab // BLOCK
    mine = ids // BLOCK
    volume = 1.0 / (length * cross)
    weights = []
    for group, sums in zip(groups, (sums_a[0], sums_a[1], sums_b)):
        listed = lax.dynamic_slice_in_dim(pattern, group * blk_slab, blk_slab, 0)
        my_blocks = slab_id * blk_slab + mine
        kept = jnp.any(listed[:, :, None] == my_blocks[None, None, :], axis=1)
        hot = jnp.arange(blk_slab, dtype=jnp.int32)[:, None] == mine[None, :]
        cover = jnp.any(kept[:, :, None] & hot[:, None, :], axis=0).astype(F32)
        inter = (sums[:per_slab] * volume * cover).astype(BF16)
        hamil = (sums[per_slab:] * volume * cover).astype(BF16)
        weights.append(jnp.concatenate([-hamil, inter], axis=1))
    weight = jnp.stack(weights)

    scale = 1.0 / (pattern.shape[1] * BLOCK)
    out_shape = (peers, narrow, held, cross)
    grad = pl.pallas_call(
        functools.partial(gradient_kernel, CHUNKS, scale),
        grid=(narrow,),
        in_specs=[whole(offs[0]), SMEM, SMEM, whole(weight)]
        + [per_col(right_shape), per_col(left_shape), per_col(left_shape)],
        out_specs=per_col(out_shape, 1),
        out_shape=jax.ShapeDtypeStruct(out_shape, BF16),
        compiler_params=PARAMS,
    )(offs[0], base, first_side.reshape(1), weight, right, one_left, two_left)
    owned = lax.all_to_all(grad, "orb", split_axis=0, concat_axis=0, tiled=True)
    owned = owned.reshape(length, held, cross).transpose(1, 0, 2)
    doubled = jnp.concatenate([owned, owned], axis=1)
    return window_rows(doubled, offset, length)


def solution(mesh):
    placed = (
        P(("slab", "orb"), None, None),
        P(("slab", "orb")),
        P(),
        P(("slab", "orb"), None),
        P(),
    )
    return jax.shard_map(
        per_device,
        mesh=mesh,
        in_specs=placed,
        out_specs=P(("slab", "orb"), None, None),
        check_vma=False,
    )
```

time: 730 us -> 483 us (0.66)
  waiting for transfers between devices: 298 us -> 150 us
  Pallas kernels: 0 us -> 112 us
  local copies, waits for them, and re-layouts: 142 us -> 40.9 us
  matrix products: 53.4 us -> 0 us
  other arithmetic: 56.3 us -> 20 us
  blocking collectives: 143 us -> 123 us
    ppermute x4 -> x5, waiting for transfers between devices: 280 us -> 68 us  [the longest x2 68 us: per_device(): one_parts.append(lax.ppermute(part, 'slab', swap))]
    pallas_call x0 -> x4, Pallas kernels: none -> 112 us  [the longest x2 58.1 us: other(): pl.pallas_call(functools.partial(other_kernel, CHUNKS, length), grid=(nar...]
    dot_general x5 -> x0, matrix products: 53.4 us -> none  [the longest x1 13.7 us: per_device(): lax.dot_general(flat_phi, flat_app, contract_rows, preferred_element_type...]
    all_to_all x1 -> x2, waiting for transfers between devices: 0.01 us -> 40.9 us  [per_device(): lax.all_to_all(cut, 'orb', split_axis=0, concat_axis=0, tiled=True)]
    psum x1, waiting for transfers between devices: 18.1 us -> 41.3 us  [per_device(): sums_b = lax.psum(two_sums, 'orb')]
    unnamed x1, blocking collectives: 92.3 us -> 69.1 us
    slice x3 -> x2, local copies, waits for them, and re-layouts: 24.8 us -> 4.95 us  [the longest x1 3.94 us: per_device(): values = orbitals[rows]]
    concatenate x4 -> x3, other arithmetic: 30.1 us -> 12.1 us  [the longest x1 7.41 us: per_device(): doubled = jnp.concatenate([owned, owned], axis=1)]
  transfers between devices with their start and end apart: 6 -> 8, of which waited for: 4 -> 5; matrix products, arithmetic and copies ran while one was open for 6% -> 3% of each run, Pallas kernels for 0% -> 11%
where the time goes in v1:
time: 483 us; the launch traced here: 480 us
  waiting for transfers between devices  150 us (31%)
  blocking collectives  123 us (25%)
  Pallas kernels  112 us (23%)
  local copies, waits for them, and re-layouts  40.9 us (8%)
  starting transfers between devices  20.1 us (4%)
  other arithmetic  20 us (4%)
  between operations  13.6 us (3%)
    unnamed x1, blocking collectives  69.1 us
    ppermute x2, waiting for transfers between devices, per_device(): one_parts.append(lax.ppermute(part, 'slab', swap))  68 us
    pallas_call x2, Pallas kernels, other(): pl.pallas_call(functools.partial(other_kernel, CHUNKS, length), grid=(nar...  58.1 us
    all_to_all x1, blocking collectives, per_device(): owned = lax.all_to_all(grad, 'orb', split_axis=0, concat_axis=0, tiled=True)  53.9 us
    psum x1, waiting for transfers between devices, per_device(): sums_b = lax.psum(two_sums, 'orb')  41.3 us
    all_to_all x2, waiting for transfers between devices, per_device(): lax.all_to_all(cut, 'orb', split_axis=0, concat_axis=0, tiled=True)  40.9 us
    gather x4, local copies, waits for them, and re-layouts, single(): return lax.dynamic_slice_in_dim(orb_row, begin_at, length, 0)  31.9 us
    pallas_call x1, Pallas kernels, per_device(): pl.pallas_call(functools.partial(gradient_kernel, CHUNKS, scale), grid=(n...  29.5 us
  transfers between devices with their start and end apart: 8, of which 5 were waited for; matrix products, arithmetic and copies ran while one was open for 3% of the time, Pallas kernels for 11%

profile of v1, /device:TPU:0, one launch (start us, length us, event | category | flops | bytes accessed | tf_op | source)
XLA Modules:
  0.0 480.0 jit_solution(17762522010105857661)
XLA Ops:
  6.5 3.9 fusion.37
  12.8 2.4 pad_maximum_fusion.2
  15.2 6.3 %gather_fusion.1 = bf16[32,130,256]{2,0,1:T(8,128)(2,1)S(1)} fusion(bf16[32,258,256]{2,0,1:T(8,128)(2,1)} %pad_maximum_fusion.2, s32[32]{0:T(128)S(1)} %get-tuple-element.51), kind=kCustom, calls=%fused_computation.1 | custom fusion | bytes 4260224 | tf_op jit(solution)/shard_map/vmap()/gather | solution.py:133
  23.3 4.8 all-to-all-start.1
  29.3 2.4 pad_maximum_fusion.1
  31.7 6.3 %gather_fusion = bf16[32,130,256]{2,0,1:T(8,128)(2,1)S(1)} fusion(bf16[32,258,256]{2,0,1:T(8,128)(2,1)} %pad_maximum_fusion.1, s32[32]{0:T(128)S(1)} %get-tuple-element.52), kind=kCustom, calls=%fused_computation | custom fusion | bytes 4260224 | tf_op jit(solution)/shard_map/vmap()/gather | solution.py:133
  39.9 16.0 %all-to-all-done.1.refs_1_ = bf16[4,34,32,256]{3,2,1,0:T(8,128)(2,1)} async-done(((bf16[4,34,32,256]{3,2,1,0:T(8,128)(2,1)}), bf16[4,34,32,256]{3,2,1,0:T(8,128)(2,1)}, u32[]{:S(2)}, u32[]{:S(2)}) %all-to-all-start.1) | async-done | bytes 2228256 | tf_op jit(solution)/shard_map/all_to_all | solution.py:177
  55.9 3.6 all-to-all-start
  59.6 2.2 collective-permute-start.2
  61.8 24.8 %all-to-all-done.refs_0_ = bf16[4,34,32,256]{3,2,1,0:T(8,128)(2,1)S(1)} async-done(((bf16[4,34,32,256]{3,2,1,0:T(8,128)(2,1)}), bf16[4,34,32,256]{3,2,1,0:T(8,128)(2,1)S(1)}, u32[]{:S(2)}, u32[]{:S(2)}) %all-to-all-start) | async-done | bytes 2228256 | tf_op jit(solution)/shard_map/all_to_all | solution.py:177
  86.6 2.1 collective-permute-start.1
  88.7 22.7 %collective-permute-done.2.refs_1_ = bf16[4,34,32,256]{3,2,1,0:T(8,128)(2,1)} collective-permute-done((bf16[4,34,32,256]{3,2,1,0:T(8,128)(2,1)}, bf16[4,34,32,256]{3,2,1,0:T(8,128)(2,1)}, u32[]{:S(2)}, u32[]{:S(2)}) %collective-permute-start.2) | collective-permute-done | bytes 2228256 | tf_op jit(solution)/shard_map/ppermute | solution.py:179
  113.5 45.4 %collective-permute-done.1.refs_0_ = bf16[4,34,32,256]{3,2,1,0:T(8,128)(2,1)} collective-permute-done((bf16[4,34,32,256]{3,2,1,0:T(8,128)(2,1)S(1)}, bf16[4,34,32,256]{3,2,1,0:T(8,128)(2,1)}, u32[]{:S(2)}, u32[]{:S(2)}) %collective-permute-start.1) | collective-permute-done | bytes 2228256 | tf_op jit(solution)/shard_map/ppermute | solution.py:179
  160.6 3.4 collective-permute-start
  164.3 69.1 %all-reduce.3 = s32[2048]{0:T(1024)S(1)} all-reduce(s32[2048]{0:T(1024)S(1)} %dynamic-update-slice), channel_id=1, replica_groups=mesh['slab'=8,'orb'=4] {'slab','orb'}, use_global_device_ids=true, to_apply=%add.3 | all-reduce | flops 2048 | bytes 16384
  234.1 24.5 %shard_map.55 = (bf16[32,2,512,256]{3,2,1,0:T(8,128)(2,1)}, f32[512,256]{1,0:T(8,128)S(1)}) custom-call(bf16[4,34,32,256]{3,2,1,0:T(8,128)(2,1)S(1)} %all-to-all-done.refs_0_, bf16[4,34,32,256]{3,2,1,0:T(8,128)(2,1)} %all-to-all-done.1.refs_1_, f32[256,256]{1,0:T(8,128)S(1)} %broadcast_in_dim.12.refs_2_.refs_0_, f32[1]{0:T(128)} %bitcast.1.refs_3_.refs_1_, ...), custom_call_target="tpu_custom_call" | custom-call | flops 5368709120 | bytes 23068672 | tf_op jit(solution)/shard_map/pallas_call | solution.py:188
  258.7 28.9 %shard_map.56 = (bf16[32,512,256]{2,1,0:T(8,128)(2,1)}, f32[512,256]{1,0:T(8,128)S(1)}) custom-call(bf16[4,34,32,256]{3,2,1,0:T(8,128)(2,1)} %collective-permute-done.1.refs_0_, bf16[4,34,32,256]{3,2,1,0:T(8,128)(2,1)} %collective-permute-done.2.refs_1_, f32[256,256]{1,0:T(8,128)S(1)} %broadcast_in_dim.15.refs_2_, f32[1]{0:T(128)} %bitcast.1.refs_3_.refs_1_, ...), custom_call_target="tpu_custom_call" | custom-call | flops 3221225472 | bytes 31457280 | tf_op jit(solution)/shard_map/pallas_call | solution.py:205
  288.8 29.2 %shard_map.57 = (bf16[32,512,256]{2,1,0:T(8,128)(2,1)}, f32[512,256]{1,0:T(8,128)}) custom-call(bf16[4,34,32,256]{3,2,1,0:T(8,128)(2,1)} %collective-permute-done.3.refs_0_, bf16[4,34,32,256]{3,2,1,0:T(8,128)(2,1)} %collective-permute-done.4.refs_1_, f32[256,256]{1,0:T(8,128)S(1)} %broadcast_in_dim.16.refs_2_, f32[1]{0:T(128)} %bitcast.1.refs_3_.refs_1_, ...), custom_call_target="tpu_custom_call" | custom-call | flops 3221225472 | bytes 31457280 | tf_op jit(solution)/shard_map/pallas_call | solution.py:205
  319.0 41.3 %all-reduce.7.cloned.1.call-done = (f32[512,256]{1,0:T(8,128)}, f32[2,512,256]{2,1,0:T(8,128)}) async-done(((f32[512,256]{1,0:T(8,128)}, f32[2,512,256]{2,1,0:T(8,128)}), (f32[512,256]{1,0:T(8,128)}, f32[2,512,256]{2,1,0:T(8,128)})) %all-reduce.7.cloned.1.call-update) | async-done | bytes 1572880 | tf_op jit(solution)/shard_map/psum | solution.py:224
  363.0 29.5 %shard_map.58 = bf16[4,32,64,256]{3,2,1,0:T(8,128)(2,1)} custom-call(f32[256,256]{1,0:T(8,128)S(1)} %broadcast_in_dim.12.refs_2_.refs_0_, f32[1]{0:T(128)} %bitcast.1.refs_3_.refs_1_, s32[1]{0:T(128)} %bitcast.2.refs_4_.refs_2_, bf16[3,256,512]{2,1,0:T(8,128)(2,1)S(1)} %pad_maximum_fusion.4.refs_3_, ...), custom_call_target="tpu_custom_call" | custom-call | tf_op jit(solution)/shard_map/pallas_call | solution.py:243
  392.4 53.9 %all_to_all.15 = bf16[4,32,64,256]{3,2,1,0:T(8,128)(2,1)} all-to-all(bf16[4,32,64,256]{3,2,1,0:T(8,128)(2,1)} %shard_map.58), channel_id=1, replica_groups=mesh['slab'=8,'orb'=4] {'orb'}, dimensions={0} | all-to-all | bytes 8388608 | tf_op jit(solution)/shard_map/all_to_all | solution.py:252
  446.3 7.4 %pad_maximum_fusion = bf16[64,256,256]{2,0,1:T(8,128)(2,1)} fusion(bf16[64,128,256]{2,0,1:T(8,128)(2,1)} %bitcast.89), kind=kLoop, calls=%fused_computation.3 | loop fusion | flops 4194304 | bytes 12582912 | tf_op jit(solution)/shard_map/concatenate | solution.py:254
  453.8 12.8 %gather_fusion.2 = bf16[64,128,256]{2,0,1:T(8,128)(2,1)} fusion(bf16[64,256,256]{2,0,1:T(8,128)(2,1)} %pad_maximum_fusion, s32[64]{0:T(128)S(1)} %get-tuple-element.28), kind=kCustom, calls=%fused_computation.2 | custom fusion | bytes 8389376 | tf_op jit(solution)/shard_map/vmap()/gather | solution.py:133
  466.5 6.6 %copy.40 = bf16[64,128,256]{2,1,0:T(8,128)(2,1)} copy(bf16[64,128,256]{2,0,1:T(8,128)(2,1)} %gather_fusion.2) | data formatting | bytes 8388608 | tf_op jit(solution)/shard_map/vmap()/gather | solution.py:133
  (59 shorter events, 16.9 us)
Async XLA Ops:
  6.5 5.0 %copy-start.4 = (s32[64]{0:T(128)S(1)}, s32[64]{0:T(128)}, u32[]{:S(2)}) copy-start(s32[64]{0:T(128)} %param.6) | copy-start | bytes 772
  23.3 4.8 copy-start.1
  23.3 32.6 %all-to-all-start.1 = ((bf16[4,34,32,256]{3,2,1,0:T(8,128)(2,1)}), bf16[4,34,32,256]{3,2,1,0:T(8,128)(2,1)}, u32[]{:S(2)}, u32[]{:S(2)}) async-start(bf16[4,34,32,256]{3,2,1,0:T(8,128)(2,1)} %maximum_bitcast_fusion.1), calls=%async_computation.1 | async-start | bytes 4456448 | tf_op jit(solution)/shard_map/all_to_all | solution.py:177
  39.9 120.8 %copy-start.3 = (f32[32,256]{1,0:T(8,128)S(1)}, f32[32,256]{1,0:T(8,128)}, u32[]{:S(2)}) copy-start(f32[32,256]{1,0:T(8,128)} %param.8) | copy-start | bytes 98308
  39.9 194.2 %copy-start = (bf16[256,256]{1,0:T(8,128)(2,1)S(1)}, bf16[256,256]{1,0:T(8,128)(2,1)}, u32[]{:S(2)}) copy-start(bf16[256,256]{1,0:T(8,128)(2,1)} %refs_5_.3) | copy-start | bytes 393220
  55.9 30.7 %all-to-all-start = ((bf16[4,34,32,256]{3,2,1,0:T(8,128)(2,1)}), bf16[4,34,32,256]{3,2,1,0:T(8,128)(2,1)S(1)}, u32[]{:S(2)}, u32[]{:S(2)}) async-start(bf16[4,34,32,256]{3,2,1,0:T(8,128)(2,1)} %maximum_bitcast_fusion), calls=%async_computation | async-start | bytes 4456448 | tf_op jit(solution)/shard_map/all_to_all | solution.py:177
  59.5 300.7 %all-reduce.7.cloned.1.call-start = ((), (), s32[]{:S(2)}) async-start(), calls=%async_computation.3 | async-start | bytes 3145728 | tf_op jit(solution)/shard_map/psum | solution.py:224
  59.6 51.8 %collective-permute-start.2 = (bf16[4,34,32,256]{3,2,1,0:T(8,128)(2,1)}, bf16[4,34,32,256]{3,2,1,0:T(8,128)(2,1)}, u32[]{:S(2)}, u32[]{:S(2)}) collective-permute-start(bf16[4,34,32,256]{3,2,1,0:T(8,128)(2,1)} %all-to-all-done.1.refs_1_), channel_id=1, source_target_pairs={{0,4},{4,0},{8,12},{12,8},{16,20},{20,16},{24,28},{28,24},{1,5},{5... | collective-permute-start | bytes 6684680 | tf_op jit(solution)/shard_map/ppermute | solution.py:179
  86.6 72.2 %collective-permute-start.1 = (bf16[4,34,32,256]{3,2,1,0:T(8,128)(2,1)S(1)}, bf16[4,34,32,256]{3,2,1,0:T(8,128)(2,1)}, u32[]{:S(2)}, u32[]{:S(2)}) collective-permute-start(bf16[4,34,32,256]{3,2,1,0:T(8,128)(2,1)S(1)} %all-to-all-done.refs_0_), channel_id=1, source_target_pairs={{0,4},{4,0},{8,12},{12,8},{16,20},{20,16},{24,28},{28,24},{1,5},{5... | collective-permute-start | bytes 6684680 | tf_op jit(solution)/shard_map/ppermute | solution.py:179
  111.4 177.3 %collective-permute-start.4 = (bf16[4,34,32,256]{3,2,1,0:T(8,128)(2,1)}, bf16[4,34,32,256]{3,2,1,0:T(8,128)(2,1)}, u32[]{:S(2)}, u32[]{:S(2)}) collective-permute-start(bf16[4,34,32,256]{3,2,1,0:T(8,128)(2,1)} %collective-permute-done.2.refs_1_), channel_id=1, source_target_pairs={{0,8},{4,28},{8,16},{12,4},{16,24},{20,12},{24,0},{28,20},{1,9},{5... | collective-permute-start | bytes 6684680 | tf_op jit(solution)/shard_map/ppermute | solution.py:181
  158.8 129.9 %collective-permute-start.3 = (bf16[4,34,32,256]{3,2,1,0:T(8,128)(2,1)}, bf16[4,34,32,256]{3,2,1,0:T(8,128)(2,1)}, u32[]{:S(2)}, u32[]{:S(2)}) collective-permute-start(bf16[4,34,32,256]{3,2,1,0:T(8,128)(2,1)} %collective-permute-done.1.refs_0_), channel_id=1, source_target_pairs={{0,8},{4,28},{8,16},{12,4},{16,24},{20,12},{24,0},{28,20},{1,9},{5... | collective-permute-start | bytes 6684680 | tf_op jit(solution)/shard_map/ppermute | solution.py:181
  160.6 73.3 %collective-permute-start = (f32[32,256]{1,0:T(8,128)S(1)}, f32[32,256]{1,0:T(8,128)S(1)}, u32[]{:S(2)}, u32[]{:S(2)}) collective-permute-start(f32[32,256]{1,0:T(8,128)S(1)} %copy-done.3), channel_id=1, source_target_pairs={{0,28},{4,0},{8,4},{12,8},{16,12},{20,16},{24,20},{28,24},{1,29},{... | collective-permute-start | bytes 98312 | tf_op jit(solution)/shard_map/ppermute | solution.py:164
  288.8 29.3 %copy-start.2 = (s32[32,5]{0,1:T(8,128)S(1)}, s32[32,5]{0,1:T(8,128)}, u32[]{:S(2)}) copy-start(s32[32,5]{0,1:T(8,128)} %param.9) | copy-start | bytes 1924
Sparse Core Ops, SparseCore 0:
  318.2 42.0 all-reduce.6

commit v2 on v1

--- a/solution.py
+++ b/solution.py
@@ -9,6 +9,7 @@
 
 BLOCK = 64
 CHUNKS = 2
+HALVES = 2
 VMEM = 50 * 1024 * 1024
 F32 = jnp.float32
 BF16 = jnp.bfloat16
@@ -37,10 +38,10 @@
 
 def own_kernel(chunks, length, *refs):
     parts = refs[:chunks]
-    off_ref, base_ref, filt_ref, pot_ref, right_ref, sums_ref = refs[chunks:]
+    base_ref, filt_ref, pot_ref, right_ref, sums_ref = refs[chunks:]
     col = pl.program_id(0)
     place = base_ref[0] + col.astype(F32)
-    off = off_ref[...]
+    off = column(parts, parts[0].shape[1] - 1).astype(F32)
     wide, kin = kinetic_of(parts, col, place, filt_ref[...], off, length)
     count = wide.shape[0]
     own = off <= place
@@ -65,10 +66,10 @@
 
 def other_kernel(chunks, length, *refs):
     parts = refs[:chunks]
-    off_ref, base_ref, side_ref, filt_ref, pot_ref, right_ref, left_ref, sums_ref = refs[chunks:]
+    base_ref, side_ref, filt_ref, pot_ref, right_ref, left_ref, sums_ref = refs[chunks:]
     col = pl.program_id(0)
     place = base_ref[0] + col.astype(F32)
-    off = off_ref[...]
+    off = column(parts, parts[0].shape[1] - 1).astype(F32)
     wide, kin = kinetic_of(parts, col, place, filt_ref[...], off, length)
     count = wide.shape[0]
     side = side_ref[0]
@@ -90,21 +91,32 @@
     )
 
 
-def gradient_kernel(chunks, scale, *refs):
-    off_ref, base_ref, side_ref, weight_ref, right_ref, one_ref, two_ref, out_ref = refs
-    col = pl.program_id(0)
-    place = base_ref[0] + col.astype(F32)
-    off = off_ref[...]
+def near_kernel(chunks, *refs):
+    parts = refs[:chunks]
+    base_ref, side_ref, weight_ref, right_ref, one_ref, sum_ref = refs[chunks:]
+    place = base_ref[0] + pl.program_id(0).astype(F32)
+    off = column(parts, parts[0].shape[1] - 1).astype(F32)
     sign = jnp.where(side_ref[0] == 0, F32(1.0), F32(-1.0))
-    own = off <= place
     with_one = (place + 0.5 - off) * sign > 0.0
 
     def product(which, block):
         return lax.dot_general(weight_ref[which], block, MAJOR, preferred_element_type=F32)
 
-    near = jnp.where(own, product(0, right_ref[0, 0]), product(0, right_ref[0, 1]))
-    far = jnp.where(with_one, product(1, one_ref[0]), product(2, two_ref[0]))
-    grad = ((near + far) * scale).astype(BF16)
+    near = jnp.where(off <= place, product(0, right_ref[0, 0]), product(0, right_ref[0, 1]))
+    far = product(1, one_ref[0])
+    sum_ref[0] = near + jnp.where(with_one, far, jnp.zeros_like(far))
+
+
+def far_kernel(chunks, begin, scale, *refs):
+    parts = refs[:chunks]
+    base_ref, side_ref, weight_ref, sum_ref, two_ref, out_ref = refs[chunks:]
+    place = base_ref[0] + (pl.program_id(0) + begin).astype(F32)
+    off = column(parts, parts[0].shape[1] - 1).astype(F32)
+    sign = jnp.where(side_ref[0] == 0, F32(1.0), F32(-1.0))
+    with_one = (place + 0.5 - off) * sign > 0.0
+    far = lax.dot_general(weight_ref[...], two_ref[0], MAJOR, preferred_element_type=F32)
+    far = jnp.where(with_one, jnp.zeros_like(far), far)
+    grad = ((sum_ref[0] + far) * scale).astype(BF16)
     peers, per = out_ref.shape[0], out_ref.shape[2] // chunks
     for chunk in range(chunks):
         for peer in range(peers):
@@ -116,9 +128,15 @@
     return pl.BlockSpec(array.shape, lambda col: (0,) * array.ndim)
 
 
-def per_col(shape, lead=0):
+def offsets_of(array):
+    shape = array.shape
+    block = (shape[0], 1) + shape[2:]
+    return pl.BlockSpec(block, lambda col: (0, shape[1] - 1, 0, 0))
+
+
+def per_col(shape, lead=0, begin=0):
     def index(col):
-        return tuple(col if at == lead else 0 for at in range(len(shape)))
+        return tuple(col + begin if at == lead else 0 for at in range(len(shape)))
 
     block = tuple(1 if at == lead else size for at, size in enumerate(shape))
     return pl.BlockSpec(block, index)
@@ -146,8 +164,6 @@
     per = held // CHUNKS
     offset = region_start - slab_id * length
 
-    starts = lax.all_gather(region_start, ("slab", "orb"), axis=0, tiled=True)
-    starts = starts.reshape(slabs, per_slab)
     ids = jnp.arange(per_slab, dtype=jnp.int32).reshape(peers, CHUNKS, per)
     ids = ids.transpose(1, 0, 2).reshape(per_slab)
     odd = slab_id % 2
@@ -155,11 +171,6 @@
     second = lax.rem(slab_id - 1 + 2 * odd + slabs, slabs)
     first_side = (1 - odd).astype(jnp.int32)
     groups = [slab_id, first, second]
-    offs = []
-    for group in groups:
-        row = lax.dynamic_index_in_dim(starts, group, 0, keepdims=False) - group * length
-        row = row.reshape(peers, CHUNKS, per).transpose(1, 0, 2).reshape(per_slab, 1)
-        offs.append(jnp.broadcast_to(row.astype(F32), (per_slab, cross)))
     base = (orb_id * narrow).astype(F32).reshape(1)
     pot_next = lax.ppermute(potential, "slab", [(i, (i - 1) % slabs) for i in range(slabs)])
     pots = jnp.stack([potential, pot_next])
@@ -173,7 +184,10 @@
         around = jnp.concatenate([values, values, values[:, :2]], axis=1)
         rolled = window_rows(around, length - 1 - offset[rows], length + 2)
         cut = jnp.stack([rolled[:, d * narrow:(d + 1) * narrow + 2] for d in range(peers)])
-        cut = cut.transpose(0, 2, 1, 3)
+        told = jnp.broadcast_to(offset[rows].astype(BF16)[None, None, :, None], (peers, 1, per, cross))
+        cut = jnp.concatenate([cut.transpose(0, 2, 1, 3), told], axis=1)
+        if chunk == 0:
+            cut, pots = lax.optimization_barrier((cut, pots))
         own_parts.append(lax.all_to_all(cut, "orb", split_axis=0, concat_axis=0, tiled=True))
     for part in own_parts:
         one_parts.append(lax.ppermute(part, "slab", swap))
@@ -189,7 +203,7 @@
         functools.partial(own_kernel, CHUNKS, length),
         grid=(narrow,),
         in_specs=[whole(p) for p in own_parts]
-        + [whole(offs[0]), SMEM, whole(kin_cross), whole(pots)],
+        + [SMEM, whole(kin_cross), whole(pots)],
         out_specs=[per_col(right_shape), sums_spec],
         out_shape=[
             jax.ShapeDtypeStruct(right_shape, BF16),
@@ -199,14 +213,14 @@
         cost_estimate=pl.CostEstimate(
             flops=5 * product, bytes_accessed=22 * 2**20, transcendentals=0
         ),
-    )(*own_parts, offs[0], base, kin_cross, pots)
-
-    def other(parts, off, side):
+    )(*own_parts, base, kin_cross, pots)
+
+    def other(parts, side):
         return pl.pallas_call(
             functools.partial(other_kernel, CHUNKS, length),
             grid=(narrow,),
             in_specs=[whole(p) for p in parts]
-            + [whole(off), SMEM, SMEM, whole(kin_cross), whole(pots), per_col(right_shape)],
+            + [SMEM, SMEM, whole(kin_cross), whole(pots), per_col(right_shape)],
             out_specs=[per_col(left_shape), sums_spec],
             out_shape=[
                 jax.ShapeDtypeStruct(left_shape, BF16),
@@ -216,11 +230,12 @@
             cost_estimate=pl.CostEstimate(
                 flops=3 * product, bytes_accessed=30 * 2**20, transcendentals=0
             ),
-        )(*parts, off, base, side.reshape(1), kin_cross, pots, right)
-
-    one_left, one_sums = other(one_parts, offs[1], first_side)
+        )(*parts, base, side.reshape(1), kin_cross, pots, right)
+
+    one_left, one_sums = other(one_parts, first_side)
     sums_a = lax.psum(jnp.stack([own_sums, one_sums]), "orb")
-    two_left, two_sums = other(two_parts, offs[2], 1 - first_side)
+    sums_a, two_parts = lax.optimization_barrier((sums_a, two_parts))
+    two_left, two_sums = other(two_parts, 1 - first_side)
     sums_b = lax.psum(two_sums, "orb")
 
     blk_slab = per_slab // BLOCK
@@ -236,20 +251,42 @@
         inter = (sums[:per_slab] * volume * cover).astype(BF16)
         hamil = (sums[per_slab:] * volume * cover).astype(BF16)
         weights.append(jnp.concatenate([-hamil, inter], axis=1))
-    weight = jnp.stack(weights)
+    weight = jnp.stack(weights[:2])
 
     scale = 1.0 / (pattern.shape[1] * BLOCK)
-    out_shape = (peers, narrow, held, cross)
-    grad = pl.pallas_call(
-        functools.partial(gradient_kernel, CHUNKS, scale),
+    told = [offsets_of(p) for p in own_parts]
+    side = first_side.reshape(1)
+    partial_shape = (narrow, per_slab, cross)
+    partial = pl.pallas_call(
+        functools.partial(near_kernel, CHUNKS),
         grid=(narrow,),
-        in_specs=[whole(offs[0]), SMEM, SMEM, whole(weight)]
-        + [per_col(right_shape), per_col(left_shape), per_col(left_shape)],
-        out_specs=per_col(out_shape, 1),
-        out_shape=jax.ShapeDtypeStruct(out_shape, BF16),
+        in_specs=told + [SMEM, SMEM, whole(weight), per_col(right_shape), per_col(left_shape)],
+        out_specs=per_col(partial_shape),
+        out_shape=jax.ShapeDtypeStruct(partial_shape, F32),
         compiler_params=PARAMS,
-    )(offs[0], base, first_side.reshape(1), weight, right, one_left, two_left)
-    owned = lax.all_to_all(grad, "orb", split_axis=0, concat_axis=0, tiled=True)
+        cost_estimate=pl.CostEstimate(
+            flops=3 * product, bytes_accessed=36 * 2**20, transcendentals=0
+        ),
+    )(*own_parts, base, side, weight, right, one_left)
+    half = narrow // HALVES
+    out_shape = (peers, half, held, cross)
+    landed = []
+    for begin in range(0, narrow, half):
+        grad = pl.pallas_call(
+            functools.partial(far_kernel, CHUNKS, begin, scale),
+            grid=(half,),
+            in_specs=told
+            + [SMEM, SMEM, whole(weights[2])]
+            + [per_col(partial_shape, 0, begin), per_col(left_shape, 0, begin)],
+            out_specs=per_col(out_shape, 1),
+            out_shape=jax.ShapeDtypeStruct(out_shape, BF16),
+            compiler_params=PARAMS,
+            cost_estimate=pl.CostEstimate(
+                flops=product // HALVES, bytes_accessed=10 * 2**20, transcendentals=0
+            ),
+        )(*own_parts, base, side, weights[2], partial, two_left)
+        landed.append(lax.all_to_all(grad, "orb", split_axis=0, concat_axis=0, tiled=True))
+    owned = jnp.concatenate(landed, axis=1)
     owned = owned.reshape(length, held, cross).transpose(1, 0, 2)
     doubled = jnp.concatenate([owned, owned], axis=1)
     return window_rows(doubled, offset, length)

time: 483 us -> 435 us (0.901)
  blocking collectives: 123 us -> 28.2 us
  Pallas kernels: 112 us -> 134 us
  waiting for transfers between devices: 150 us -> 162 us
  starting transfers between devices: 20.1 us -> 27.6 us
  other arithmetic: 20 us -> 26.9 us
    unnamed x1 -> x0, blocking collectives: 69.1 us -> none
    psum x0 -> x1, waiting for transfers between devices: none -> 35.7 us  [per_device(): sums_a = lax.psum(jnp.stack([own_sums, one_sums]), 'orb')]
    psum x1, waiting for transfers between devices: 41.3 us -> 5.98 us  [per_device(): sums_b = lax.psum(two_sums, 'orb')]
    all_to_all x1, blocking collectives: 53.9 us -> 28.2 us  [per_device(): lax.all_to_all(grad, 'orb', split_axis=0, concat_axis=0, tiled=True)]
    pallas_call x1 -> x3, Pallas kernels: 29.5 us -> 50.6 us  [the longest x1 27.6 us: per_device(): pl.pallas_call(functools.partial(near_kernel, CHUNKS), grid=(narrow,), in...]
    all_to_all x0 -> x1, waiting for transfers between devices: none -> 14.9 us  [per_device(): lax.all_to_all(grad, 'orb', split_axis=0, concat_axis=0, tiled=True)]
    concatenate x0 -> x4, other arithmetic: none -> 7.19 us  [the longest x1 3.96 us: per_device(): owned = jnp.concatenate(landed, axis=1)]
    all_to_all x2, waiting for transfers between devices: 40.9 us -> 35.6 us  [per_device(): lax.all_to_all(cut, 'orb', split_axis=0, concat_axis=0, tiled=True)]
  transfers between devices with their start and end apart: 8 -> 10, of which waited for: 5 -> 7; matrix products, arithmetic and copies ran while one was open for 3% -> 3% of each run, Pallas kernels for 11% -> 21%
where the time goes in v2:
time: 435 us; the launch traced here: 432 us
  waiting for transfers between devices  162 us (37%)
  Pallas kernels  134 us (31%)
  local copies, waits for them, and re-layouts  40.2 us (9%)
  blocking collectives  28.2 us (6%)
  starting transfers between devices  27.6 us (6%)
  other arithmetic  26.9 us (6%)
  between operations  13.6 us (3%)
    ppermute x2, waiting for transfers between devices, per_device(): one_parts.append(lax.ppermute(part, 'slab', swap))  70.1 us
    pallas_call x2, Pallas kernels, other(): pl.pallas_call(functools.partial(other_kernel, CHUNKS, length), grid=(nar...  58.5 us
    psum x1, waiting for transfers between devices, per_device(): sums_a = lax.psum(jnp.stack([own_sums, one_sums]), 'orb')  35.7 us
    all_to_all x2, waiting for transfers between devices, per_device(): lax.all_to_all(cut, 'orb', split_axis=0, concat_axis=0, tiled=True)  35.6 us
    gather x4, local copies, waits for them, and re-layouts, single(): return lax.dynamic_slice_in_dim(orb_row, begin_at, length, 0)  31.9 us
    all_to_all x1, blocking collectives, per_device(): lax.all_to_all(grad, 'orb', split_axis=0, concat_axis=0, tiled=True)  28.2 us
    pallas_call x1, Pallas kernels, per_device(): pl.pallas_call(functools.partial(near_kernel, CHUNKS), grid=(narrow,), in...  27.6 us
    pallas_call x1, Pallas kernels, per_device(): pl.pallas_call(functools.partial(own_kernel, CHUNKS, length), grid=(narro...  24.7 us
  transfers between devices with their start and end apart: 10, of which 7 were waited for; matrix products, arithmetic and copies ran while one was open for 3% of the time, Pallas kernels for 21%

profile of v2, /device:TPU:0, one launch (start us, length us, event | category | flops | bytes accessed | tf_op | source)
XLA Modules:
  0.0 432.4 jit_solution(9071785447319826115)
XLA Ops:
  8.4 4.0 fusion.20
  15.9 6.3 %gather_fusion.1 = bf16[32,130,256]{2,0,1:T(8,128)(2,1)S(1)} fusion(bf16[32,258,256]{2,0,1:T(8,128)(2,1)} %pad_maximum_fusion.2, s32[32]{0:T(128)S(1)} %get-tuple-element.56), kind=kCustom, calls=%fused_computation.1 | custom fusion | bytes 4260224 | tf_op jit(solution)/shard_map/vmap()/gather | solution.py:151
  24.5 4.6 %all-to-all-start.1 = ((bf16[4,35,32,256]{3,2,1,0:T(8,128)(2,1)}), bf16[4,35,32,256]{3,2,1,0:T(8,128)(2,1)}, u32[]{:S(2)}, u32[]{:S(2)}) async-start(bf16[4,35,32,256]{3,2,1,0:T(8,128)(2,1)} %pad_maximum_fusion.5), calls=%async_computation.1 | async-start | bytes 4587520 | tf_op jit(solution)/shard_map/all_to_all | solution.py:191
  29.1 6.2 %collective-permute-start = (f32[32,256]{1,0:T(8,128)S(1)}, f32[32,256]{1,0:T(8,128)S(1)}, u32[]{:S(2)}, u32[]{:S(2)}) collective-permute-start(f32[32,256]{1,0:T(8,128)S(1)} %copy-done.4), channel_id=1, source_target_pairs={{0,28},{4,0},{8,4},{12,8},{16,12},{20,16},{24,20},{28,24},{1,29},{... | collective-permute-start | bytes 98312 | tf_op jit(solution)/shard_map/ppermute | solution.py:175
  38.8 6.3 %gather_fusion = bf16[32,130,256]{2,0,1:T(8,128)(2,1)S(1)} fusion(bf16[32,258,256]{2,0,1:T(8,128)(2,1)} %pad_maximum_fusion.1, s32[32]{0:T(128)S(1)} %get-tuple-element.57), kind=kCustom, calls=%fused_computation | custom fusion | bytes 4260224 | tf_op jit(solution)/shard_map/vmap()/gather | solution.py:151
  47.3 10.2 %all-to-all-done.1.refs_1_ = bf16[4,35,32,256]{3,2,1,0:T(8,128)(2,1)} async-done(((bf16[4,35,32,256]{3,2,1,0:T(8,128)(2,1)}), bf16[4,35,32,256]{3,2,1,0:T(8,128)(2,1)}, u32[]{:S(2)}, u32[]{:S(2)}) %all-to-all-start.1) | async-done | bytes 2293792 | tf_op jit(solution)/shard_map/all_to_all | solution.py:191
  63.7 25.3 %all-to-all-done.refs_0_ = bf16[4,35,32,256]{3,2,1,0:T(8,128)(2,1)S(1)} async-done(((bf16[4,35,32,256]{3,2,1,0:T(8,128)(2,1)}), bf16[4,35,32,256]{3,2,1,0:T(8,128)(2,1)S(1)}, u32[]{:S(2)}, u32[]{:S(2)}) %all-to-all-start) | async-done | bytes 2293792 | tf_op jit(solution)/shard_map/all_to_all | solution.py:191
  91.3 23.4 %collective-permute-done.2.refs_1_ = bf16[4,35,32,256]{3,2,1,0:T(8,128)(2,1)} collective-permute-done((bf16[4,35,32,256]{3,2,1,0:T(8,128)(2,1)}, bf16[4,35,32,256]{3,2,1,0:T(8,128)(2,1)}, u32[]{:S(2)}, u32[]{:S(2)}) %collective-permute-start.2) | collective-permute-done | bytes 2293792 | tf_op jit(solution)/shard_map/ppermute | solution.py:193
  116.7 46.8 %collective-permute-done.1.refs_0_ = bf16[4,35,32,256]{3,2,1,0:T(8,128)(2,1)} collective-permute-done((bf16[4,35,32,256]{3,2,1,0:T(8,128)(2,1)S(1)}, bf16[4,35,32,256]{3,2,1,0:T(8,128)(2,1)}, u32[]{:S(2)}, u32[]{:S(2)}) %collective-permute-start.1) | collective-permute-done | bytes 2293792 | tf_op jit(solution)/shard_map/ppermute | solution.py:193
  165.4 24.7 %shard_map.55 = (bf16[32,2,512,256]{3,2,1,0:T(8,128)(2,1)}, f32[512,256]{1,0:T(8,128)S(1)}) custom-call(bf16[4,35,32,256]{3,2,1,0:T(8,128)(2,1)S(1)} %all-to-all-done.refs_0_, bf16[4,35,32,256]{3,2,1,0:T(8,128)(2,1)} %all-to-all-done.1.refs_1_, f32[1]{0:T(128)} %bitcast.16.refs_2_, bf16[256,256]{1,0:T(8,128)(2,1)S(1)} %copy-done.1, ...), custom_call_target="tpu_custom_call" | custom-call | flops 5368709120 | bytes 23068672 | tf_op jit(solution)/shard_map/pallas_call | solution.py:202
  190.1 29.0 %shard_map.56 = (bf16[32,512,256]{2,1,0:T(8,128)(2,1)}, f32[512,256]{1,0:T(8,128)S(1)}) custom-call(bf16[4,35,32,256]{3,2,1,0:T(8,128)(2,1)} %collective-permute-done.1.refs_0_, bf16[4,35,32,256]{3,2,1,0:T(8,128)(2,1)} %collective-permute-done.2.refs_1_, f32[1]{0:T(128)} %bitcast.16.refs_2_, s32[1]{0:T(128)} %bitcast.17.refs_3_, ...), custom_call_target="tpu_custom_call" | custom-call | flops 3221225472 | bytes 31457280 | tf_op jit(solution)/shard_map/pallas_call | solution.py:219
  221.2 35.7 %all-reduce.6.cloned.1.call-done = f32[2,512,256]{2,1,0:T(8,128)} async-done(((f32[2,512,256]{2,1,0:T(8,128)}), f32[2,512,256]{2,1,0:T(8,128)}) %all-reduce.6.cloned.1.call-update) | async-done | bytes 1048592 | tf_op jit(solution)/shard_map/psum | solution.py:236
  259.1 29.4 %shard_map.57 = (bf16[32,512,256]{2,1,0:T(8,128)(2,1)}, f32[512,256]{1,0:T(8,128)}) custom-call(bf16[4,35,32,256]{3,2,1,0:T(8,128)(2,1)} %collective-permute-done.3.refs_0_, bf16[4,35,32,256]{3,2,1,0:T(8,128)(2,1)} %collective-permute-done.4.refs_1_, f32[1]{0:T(128)} %bitcast.16.refs_2_, s32[1]{0:T(128)} %bitcast.20.refs_3_, bf16[256,256]{1,0:T(8,128)(2,1)S(1)} %copy-done.1, ...), custom_call_target="tpu_custom_call" | custom-call | flops 3221225472 | bytes 31457280 | tf_op jit(solution)/shard_map/pallas_call | solution.py:219
  288.7 27.6 %shard_map.58.refs_5_ = f32[32,256,256]{2,1,0:T(8,128)} custom-call(bf16[4,35,32,256]{3,2,1,0:T(8,128)(2,1)S(1)} %all-to-all-done.refs_0_, bf16[4,35,32,256]{3,2,1,0:T(8,128)(2,1)} %all-to-all-done.1.refs_1_, f32[1]{0:T(128)} %bitcast.16.refs_2_, s32[1]{0:T(128)} %bitcast.17.refs_3_, bf16[2,256,512]{2,1,0:T(8,128)(2,1)S(1)} %pad_maximum_fusion.7.refs_4_, ...), custom_call_target="tpu_custom_call" | custom-call | flops 3221225472 | bytes 37748736 | tf_op jit(solution)/shard_map/pallas_call | solution.py:260
  316.3 6.0 %all-reduce.8.cloned.1.call-done = f32[512,256]{1,0:T(8,128)} async-done(((f32[512,256]{1,0:T(8,128)}), f32[512,256]{1,0:T(8,128)}) %all-reduce.8.cloned.1.call-update) | async-done | bytes 524304 | tf_op jit(solution)/shard_map/psum | solution.py:239
  324.3 12.1 %shard_map.59 = bf16[4,16,64,256]{3,2,1,0:T(8,128)(2,1)} custom-call(bf16[4,35,32,256]{3,2,1,0:T(8,128)(2,1)} %copy-done, bf16[4,35,32,256]{3,2,1,0:T(8,128)(2,1)} %all-to-all-done.1.refs_1_, f32[1]{0:T(128)} %bitcast.16.refs_2_, s32[1]{0:T(128)} %bitcast.17.refs_3_, bf16[256,512]{1,0:T(8,128)(2,1)S(1)} %pad_maximum_fusion.8.refs_4_, ...), custom_call_target="tpu_custom_call" | custom-call | flops 536870912 | bytes 10485760 | tf_op jit(solution)/shard_map/pallas_call | solution.py:275
  336.4 4.5 %all-to-all-start.2 = ((bf16[4,16,64,256]{3,2,1,0:T(8,128)(2,1)}), bf16[4,16,64,256]{3,2,1,0:T(8,128)(2,1)}, u32[]{:S(2)}, u32[]{:S(2)}) async-start(bf16[4,16,64,256]{3,2,1,0:T(8,128)(2,1)} %shard_map.59), calls=%async_computation.2 | async-start | bytes 4194304 | tf_op jit(solution)/shard_map/all_to_all | solution.py:288
  340.9 10.9 %shard_map.60 = bf16[4,16,64,256]{3,2,1,0:T(8,128)(2,1)S(1)} custom-call(bf16[4,35,32,256]{3,2,1,0:T(8,128)(2,1)} %copy-done, bf16[4,35,32,256]{3,2,1,0:T(8,128)(2,1)} %all-to-all-done.1.refs_1_, f32[1]{0:T(128)} %bitcast.16.refs_2_, s32[1]{0:T(128)} %bitcast.17.refs_3_, bf16[256,512]{1,0:T(8,128)(2,1)S(1)} %pad_maximum_fusion.8.refs_4_, ...), custom_call_target="tpu_custom_call" | custom-call | flops 536870912 | bytes 10485760 | tf_op jit(solution)/shard_map/pallas_call | solution.py:275
  351.8 14.9 %all-to-all-done.2 = bf16[4,16,64,256]{3,2,1,0:T(8,128)(2,1)} async-done(((bf16[4,16,64,256]{3,2,1,0:T(8,128)(2,1)}), bf16[4,16,64,256]{3,2,1,0:T(8,128)(2,1)}, u32[]{:S(2)}, u32[]{:S(2)}) %all-to-all-start.2) | async-done | bytes 2097184 | tf_op jit(solution)/shard_map/all_to_all | solution.py:288
  366.6 28.2 %all_to_all.20 = bf16[4,16,64,256]{3,2,1,0:T(8,128)(2,1)S(1)} all-to-all(bf16[4,16,64,256]{3,2,1,0:T(8,128)(2,1)S(1)} %shard_map.60), channel_id=1, replica_groups=mesh['slab'=8,'orb'=4] {'orb'}, dimensions={0} | all-to-all | bytes 4194304 | tf_op jit(solution)/shard_map/all_to_all | solution.py:288
  394.8 4.0 pad_maximum_fusion.3
  398.8 7.4 %pad_maximum_fusion = bf16[64,256,256]{2,0,1:T(8,128)(2,1)} fusion(bf16[64,128,256]{2,0,1:T(8,128)(2,1)} %bitcast.76), kind=kLoop, calls=%fused_computation.3 | loop fusion | flops 4194304 | bytes 12582912 | tf_op jit(solution)/shard_map/concatenate | solution.py:291
  406.2 12.8 %gather_fusion.2 = bf16[64,128,256]{2,0,1:T(8,128)(2,1)} fusion(bf16[64,256,256]{2,0,1:T(8,128)(2,1)} %pad_maximum_fusion, s32[64]{0:T(128)S(1)} %get-tuple-element.33), kind=kCustom, calls=%fused_computation.2 | custom fusion | bytes 8389376 | tf_op jit(solution)/shard_map/vmap()/gather | solution.py:151
  418.9 6.6 %copy.18 = bf16[64,128,256]{2,1,0:T(8,128)(2,1)} copy(bf16[64,128,256]{2,0,1:T(8,128)(2,1)} %gather_fusion.2) | data formatting | bytes 8388608 | tf_op jit(solution)/shard_map/vmap()/gather | solution.py:151
  (56 shorter events, 32.0 us)
Async XLA Ops:
  24.5 4.6 %copy-start.4 = (f32[32,256]{1,0:T(8,128)S(1)}, f32[32,256]{1,0:T(8,128)}, u32[]{:S(2)}) copy-start(f32[32,256]{1,0:T(8,128)} %param.8) | copy-start | bytes 98308
  24.5 10.9 %copy-start.2 = (bf16[32,128,256]{2,1,0:T(8,128)(2,1)S(1)}, bf16[32,128,256]{2,1,0:T(8,128)(2,1)}, u32[]{:S(2)}) copy-start(bf16[32,128,256]{2,1,0:T(8,128)(2,1)} %get-tuple-element.38) | copy-start | bytes 6291460
  24.5 33.1 %all-to-all-start.1 = ((bf16[4,35,32,256]{3,2,1,0:T(8,128)(2,1)}), bf16[4,35,32,256]{3,2,1,0:T(8,128)(2,1)}, u32[]{:S(2)}, u32[]{:S(2)}) async-start(bf16[4,35,32,256]{3,2,1,0:T(8,128)(2,1)} %pad_maximum_fusion.5), calls=%async_computation.1 | async-start | bytes 4587520 | tf_op jit(solution)/shard_map/all_to_all | solution.py:191
  29.1 18.2 %collective-permute-start = (f32[32,256]{1,0:T(8,128)S(1)}, f32[32,256]{1,0:T(8,128)S(1)}, u32[]{:S(2)}, u32[]{:S(2)}) collective-permute-start(f32[32,256]{1,0:T(8,128)S(1)} %copy-done.4), channel_id=1, source_target_pairs={{0,28},{4,0},{8,4},{12,8},{16,12},{20,16},{24,20},{28,24},{1,29},{... | collective-permute-start | bytes 98312 | tf_op jit(solution)/shard_map/ppermute | solution.py:175
  47.3 118.1 %copy-start.1 = (bf16[256,256]{1,0:T(8,128)(2,1)S(1)}, bf16[256,256]{1,0:T(8,128)(2,1)}, u32[]{:S(2)}) copy-start(bf16[256,256]{1,0:T(8,128)(2,1)} %refs_4_.3) | copy-start | bytes 393220
  57.6 31.4 %all-to-all-start = ((bf16[4,35,32,256]{3,2,1,0:T(8,128)(2,1)}), bf16[4,35,32,256]{3,2,1,0:T(8,128)(2,1)S(1)}, u32[]{:S(2)}, u32[]{:S(2)}) async-start(bf16[4,35,32,256]{3,2,1,0:T(8,128)(2,1)} %pad_maximum_fusion.4), calls=%async_computation | async-start | bytes 4587520 | tf_op jit(solution)/shard_map/all_to_all | solution.py:191
  61.2 195.6 %all-reduce.6.cloned.1.call-start = ((), (), s32[]{:S(2)}) async-start(), calls=%async_computation.4 | async-start | bytes 2097152 | tf_op jit(solution)/shard_map/psum | solution.py:236
  61.3 53.4 %collective-permute-start.2 = (bf16[4,35,32,256]{3,2,1,0:T(8,128)(2,1)}, bf16[4,35,32,256]{3,2,1,0:T(8,128)(2,1)}, u32[]{:S(2)}, u32[]{:S(2)}) collective-permute-start(bf16[4,35,32,256]{3,2,1,0:T(8,128)(2,1)} %all-to-all-done.1.refs_1_), channel_id=1, source_target_pairs={{0,4},{4,0},{8,12},{12,8},{16,20},{20,16},{24,28},{28,24},{1,5},{5... | collective-permute-start | bytes 6881288 | tf_op jit(solution)/shard_map/ppermute | solution.py:193
  89.0 199.7 %copy-start = (bf16[4,35,32,256]{3,2,1,0:T(8,128)(2,1)}, bf16[4,35,32,256]{3,2,1,0:T(8,128)(2,1)S(1)}, u32[]{:S(2)}) copy-start(bf16[4,35,32,256]{3,2,1,0:T(8,128)(2,1)S(1)} %all-to-all-done.refs_0_) | copy-start | bytes 6881284
  89.0 74.5 %collective-permute-start.1 = (bf16[4,35,32,256]{3,2,1,0:T(8,128)(2,1)S(1)}, bf16[4,35,32,256]{3,2,1,0:T(8,128)(2,1)}, u32[]{:S(2)}, u32[]{:S(2)}) collective-permute-start(bf16[4,35,32,256]{3,2,1,0:T(8,128)(2,1)S(1)} %all-to-all-done.refs_0_), channel_id=1, source_target_pairs={{0,4},{4,0},{8,12},{12,8},{16,20},{20,16},{24,28},{28,24},{1,5},{5... | collective-permute-start | bytes 6881288 | tf_op jit(solution)/shard_map/ppermute | solution.py:193
  114.7 142.2 %collective-permute-start.4 = (bf16[4,35,32,256]{3,2,1,0:T(8,128)(2,1)}, bf16[4,35,32,256]{3,2,1,0:T(8,128)(2,1)}, u32[]{:S(2)}, u32[]{:S(2)}) collective-permute-start(bf16[4,35,32,256]{3,2,1,0:T(8,128)(2,1)} %collective-permute-done.2.refs_1_), channel_id=1, source_target_pairs={{0,8},{4,28},{8,16},{12,4},{16,24},{20,12},{24,0},{28,20},{1,9},{5... | collective-permute-start | bytes 6881288 | tf_op jit(solution)/shard_map/ppermute | solution.py:195
  163.5 93.4 %collective-permute-start.3 = (bf16[4,35,32,256]{3,2,1,0:T(8,128)(2,1)}, bf16[4,35,32,256]{3,2,1,0:T(8,128)(2,1)}, u32[]{:S(2)}, u32[]{:S(2)}) collective-permute-start(bf16[4,35,32,256]{3,2,1,0:T(8,128)(2,1)} %collective-permute-done.1.refs_0_), channel_id=1, source_target_pairs={{0,8},{4,28},{8,16},{12,4},{16,24},{20,12},{24,0},{28,20},{1,9},{5... | collective-permute-start | bytes 6881288 | tf_op jit(solution)/shard_map/ppermute | solution.py:195
  219.2 1.2 copy-start.3
  220.3 102.0 %all-reduce.8.cloned.1.call-start = ((), (), s32[]{:S(2)}) async-start(), calls=%async_computation.5 | async-start | bytes 1048576 | tf_op jit(solution)/shard_map/psum | solution.py:239
  336.4 30.3 %all-to-all-start.2 = ((bf16[4,16,64,256]{3,2,1,0:T(8,128)(2,1)}), bf16[4,16,64,256]{3,2,1,0:T(8,128)(2,1)}, u32[]{:S(2)}, u32[]{:S(2)}) async-start(bf16[4,16,64,256]{3,2,1,0:T(8,128)(2,1)} %shard_map.59), calls=%async_computation.2 | async-start | bytes 4194304 | tf_op jit(solution)/shard_map/all_to_all | solution.py:288
Sparse Core Ops, SparseCore 0:
  220.4 36.4 all-reduce.5
  288.7 33.5 all-reduce.7

commit v3 on v2

--- a/solution.py
+++ b/solution.py
@@ -9,7 +9,8 @@
 
 BLOCK = 64
 CHUNKS = 2
-HALVES = 2
+HALVES = 4
+GROUP = 16
 VMEM = 50 * 1024 * 1024
 F32 = jnp.float32
 BF16 = jnp.bfloat16
@@ -124,6 +125,17 @@
             out_ref[peer, 0, chunk * per:(chunk + 1) * per, :] = grad[at:at + per]
 
 
+def back_kernel(group, offset_ref, *refs):
+    out_ref = refs[-1]
+    block = jnp.concatenate([ref[...] for ref in refs[:-1]], axis=1)
+    length = out_ref.shape[1]
+    block = block.reshape(length, group, out_ref.shape[2]).astype(F32)
+    turned = jnp.swapaxes(block, 0, 1)
+    for orb in range(group):
+        back = lax.rem(length - offset_ref[pl.program_id(0) * group + orb], length)
+        out_ref[orb] = pltpu.roll(turned[orb], back, 0).astype(BF16)
+
+
 def whole(array):
     return pl.BlockSpec(array.shape, lambda col: (0,) * array.ndim)
 
@@ -191,8 +203,6 @@
         own_parts.append(lax.all_to_all(cut, "orb", split_axis=0, concat_axis=0, tiled=True))
     for part in own_parts:
         one_parts.append(lax.ppermute(part, "slab", swap))
-    for part in one_parts:
-        two_parts.append(lax.ppermute(part, "slab", onward))
 
     right_shape = (narrow, 2, 2 * per_slab, cross)
     left_shape = (narrow, 2 * per_slab, cross)
@@ -214,6 +224,11 @@
             flops=5 * product, bytes_accessed=22 * 2**20, transcendentals=0
         ),
     )(*own_parts, base, kin_cross, pots)
+
+    one_parts[0], own_sums = lax.optimization_barrier((one_parts[0], own_sums))
+    one_parts[1], right = lax.optimization_barrier((one_parts[1], right))
+    for part in one_parts:
+        two_parts.append(lax.ppermute(part, "slab", onward))
 
     def other(parts, side):
         return pl.pallas_call(
@@ -286,10 +301,16 @@
             ),
         )(*own_parts, base, side, weights[2], partial, two_left)
         landed.append(lax.all_to_all(grad, "orb", split_axis=0, concat_axis=0, tiled=True))
-    owned = jnp.concatenate(landed, axis=1)
-    owned = owned.reshape(length, held, cross).transpose(1, 0, 2)
-    doubled = jnp.concatenate([owned, owned], axis=1)
-    return window_rows(doubled, offset, length)
+    group = min(GROUP, held)
+    taken = (peers, half, group, cross)
+    return pl.pallas_call(
+        functools.partial(back_kernel, group),
+        grid=(held // group,),
+        in_specs=[SMEM] + [pl.BlockSpec(taken, lambda at: (0, 0, at, 0))] * HALVES,
+        out_specs=pl.BlockSpec((group, length, cross), lambda at: (at, 0, 0)),
+        out_shape=jax.ShapeDtypeStruct(orbitals.shape, BF16),
+        compiler_params=PARAMS,
+    )(offset, *landed)
 
 
 def solution(mesh):

time: 435 us -> 398 us (0.915)
  waiting for transfers between devices: 162 us -> 143 us
  other arithmetic: 26.9 us -> 15.5 us
  blocking collectives: 28.2 us -> 17.9 us
  local copies, waits for them, and re-layouts: 40.2 us -> 30.5 us
  starting transfers between devices: 27.6 us -> 34.5 us
  Pallas kernels: 134 us -> 140 us
    ppermute x2, waiting for transfers between devices: 70.1 us -> 46.1 us  [per_device(): one_parts.append(lax.ppermute(part, 'slab', swap))]
    gather x4 -> x2, local copies, waits for them, and re-layouts: 31.9 us -> 13.9 us  [single(): return lax.dynamic_slice_in_dim(orb_row, begin_at, length, 0)]
    concatenate x2 -> x0, other arithmetic: 11.4 us -> none  [the longest x1 7.4 us: per_device(): doubled = jnp.concatenate([owned, owned], axis=1)]
    all_to_all x1, blocking collectives: 28.2 us -> 17.9 us  [per_device(): lax.all_to_all(grad, 'orb', split_axis=0, concat_axis=0, tiled=True)]
    all_to_all x1 -> x3, waiting for transfers between devices: 14.9 us -> 23.9 us  [per_device(): lax.all_to_all(grad, 'orb', split_axis=0, concat_axis=0, tiled=True)]
    all_to_all x1 -> x3, starting transfers between devices: 4.49 us -> 12.8 us  [per_device(): lax.all_to_all(grad, 'orb', split_axis=0, concat_axis=0, tiled=True)]
    unnamed x14 -> x20, local copies, waits for them, and re-layouts: 2.41 us -> 9.29 us
    pallas_call x0 -> x1, Pallas kernels: none -> 6.88 us  [per_device(): pl.pallas_call(functools.partial(back_kernel, group), grid=(held // group...]
  transfers between devices with their start and end apart: 10 -> 12, of which waited for: 7 -> 8; matrix products, arithmetic and copies ran while one was open for 3% -> 5% of each run, Pallas kernels for 21% -> 25%
where the time goes in v3:
time: 398 us; the launch traced here: 394 us
  waiting for transfers between devices  143 us (36%)
  Pallas kernels  140 us (35%)
  starting transfers between devices  34.5 us (9%)
  local copies, waits for them, and re-layouts  30.5 us (8%)
  blocking collectives  17.9 us (4%)
  other arithmetic  15.5 us (4%)
  between operations  13.6 us (3%)
    pallas_call x2, Pallas kernels, other(): pl.pallas_call(functools.partial(other_kernel, CHUNKS, length), grid=(nar...  58.5 us
    ppermute x2, waiting for transfers between devices, per_device(): one_parts.append(lax.ppermute(part, 'slab', swap))  46.1 us
    psum x1, waiting for transfers between devices, per_device(): sums_a = lax.psum(jnp.stack([own_sums, one_sums]), 'orb')  35.5 us
    all_to_all x2, waiting for transfers between devices, per_device(): lax.all_to_all(cut, 'orb', split_axis=0, concat_axis=0, tiled=True)  31.1 us
    pallas_call x1, Pallas kernels, per_device(): pl.pallas_call(functools.partial(near_kernel, CHUNKS), grid=(narrow,), in...  27.6 us
    pallas_call x1, Pallas kernels, per_device(): pl.pallas_call(functools.partial(own_kernel, CHUNKS, length), grid=(narro...  24.5 us
    all_to_all x3, waiting for transfers between devices, per_device(): lax.all_to_all(grad, 'orb', split_axis=0, concat_axis=0, tiled=True)  23.9 us
    pallas_call x4, Pallas kernels, per_device(): pl.pallas_call(functools.partial(far_kernel, CHUNKS, begin, scale), grid=...  22.2 us
  transfers between devices with their start and end apart: 12, of which 8 were waited for; matrix products, arithmetic and copies ran while one was open for 5% of the time, Pallas kernels for 25%

profile of v3, /device:TPU:0, one launch (start us, length us, event | category | flops | bytes accessed | tf_op | source)
XLA Modules:
  0.0 394.4 jit_solution(5029150856338371024)
XLA Ops:
  15.9 6.3 %gather_fusion.1 = bf16[32,130,256]{2,0,1:T(8,128)(2,1)S(1)} fusion(bf16[32,258,256]{2,0,1:T(8,128)(2,1)} %pad_maximum_fusion.1, s32[32]{0:T(128)S(1)} %get-tuple-element.62), kind=kCustom, calls=%fused_computation.1 | custom fusion | bytes 4260224 | tf_op jit(solution)/shard_map/vmap()/gather | solution.py:163
  24.4 4.4 %all-to-all-start.1 = ((bf16[4,35,32,256]{3,2,1,0:T(8,128)(2,1)}), bf16[4,35,32,256]{3,2,1,0:T(8,128)(2,1)S(1)}, u32[]{:S(2)}, u32[]{:S(2)}) async-start(bf16[4,35,32,256]{3,2,1,0:T(8,128)(2,1)} %pad_maximum_fusion.3), calls=%async_computation.1 | async-start | bytes 4587520 | tf_op jit(solution)/shard_map/all_to_all | solution.py:203
  28.8 5.6 %collective-permute-start = (f32[32,256]{1,0:T(8,128)S(1)}, f32[32,256]{1,0:T(8,128)S(1)}, u32[]{:S(2)}, u32[]{:S(2)}) collective-permute-start(f32[32,256]{1,0:T(8,128)S(1)} %copy-done.7), channel_id=1, source_target_pairs={{0,28},{4,0},{8,4},{12,8},{16,12},{20,16},{24,20},{28,24},{1,29},{... | collective-permute-start | bytes 98312 | tf_op jit(solution)/shard_map/ppermute | solution.py:187
  39.5 7.6 %gather_fusion = bf16[32,130,256]{2,0,1:T(8,128)(2,1)} fusion(bf16[32,258,256]{2,0,1:T(8,128)(2,1)} %pad_maximum_fusion, s32[32]{0:T(128)S(1)} %get-tuple-element.63), kind=kCustom, calls=%fused_computation | custom fusion | bytes 4260224 | tf_op jit(solution)/shard_map/vmap()/gather | solution.py:163
  50.8 5.7 %all-to-all-done.1.refs_1_ = bf16[4,35,32,256]{3,2,1,0:T(8,128)(2,1)S(1)} async-done(((bf16[4,35,32,256]{3,2,1,0:T(8,128)(2,1)}), bf16[4,35,32,256]{3,2,1,0:T(8,128)(2,1)S(1)}, u32[]{:S(2)}, u32[]{:S(2)}) %all-to-all-start.1) | async-done | bytes 2293792 | tf_op jit(solution)/shard_map/all_to_all | solution.py:203
  64.1 25.3 %all-to-all-done.refs_0_ = bf16[4,35,32,256]{3,2,1,0:T(8,128)(2,1)S(1)} async-done(((bf16[4,35,32,256]{3,2,1,0:T(8,128)(2,1)}), bf16[4,35,32,256]{3,2,1,0:T(8,128)(2,1)S(1)}, u32[]{:S(2)}, u32[]{:S(2)}) %all-to-all-start) | async-done | bytes 2293792 | tf_op jit(solution)/shard_map/all_to_all | solution.py:203
  91.7 24.5 %shard_map.55 = (bf16[32,2,512,256]{3,2,1,0:T(8,128)(2,1)}, f32[512,256]{1,0:T(8,128)S(1)}) custom-call(bf16[4,35,32,256]{3,2,1,0:T(8,128)(2,1)S(1)} %all-to-all-done.refs_0_, bf16[4,35,32,256]{3,2,1,0:T(8,128)(2,1)} %copy-done.5, f32[1]{0:T(128)} %bitcast.16.refs_2_, bf16[256,256]{1,0:T(8,128)(2,1)S(1)} %copy-done.4, ...), custom_call_target="tpu_custom_call" | custom-call | flops 5368709120 | bytes 23068672 | tf_op jit(solution)/shard_map/pallas_call | solution.py:212
  117.8 46.1 %collective-permute-done.1.refs_0_ = bf16[4,35,32,256]{3,2,1,0:T(8,128)(2,1)} collective-permute-done((bf16[4,35,32,256]{3,2,1,0:T(8,128)(2,1)S(1)}, bf16[4,35,32,256]{3,2,1,0:T(8,128)(2,1)}, u32[]{:S(2)}, u32[]{:S(2)}) %collective-permute-start.1) | collective-permute-done | bytes 2293792 | tf_op jit(solution)/shard_map/ppermute | solution.py:205
  165.8 29.1 %shard_map.56 = (bf16[32,512,256]{2,1,0:T(8,128)(2,1)}, f32[512,256]{1,0:T(8,128)S(1)}) custom-call(bf16[4,35,32,256]{3,2,1,0:T(8,128)(2,1)} %collective-permute-done.1.refs_0_, bf16[4,35,32,256]{3,2,1,0:T(8,128)(2,1)} %collective-permute-done.2.refs_1_, f32[1]{0:T(128)} %bitcast.16.refs_2_, s32[1]{0:T(128)} %bitcast.17.refs_3_, ...), custom_call_target="tpu_custom_call" | custom-call | flops 3221225472 | bytes 31457280 | tf_op jit(solution)/shard_map/pallas_call | solution.py:234
  196.9 35.5 %all-reduce.5.cloned.1.call-done = f32[2,512,256]{2,1,0:T(8,128)} async-done(((f32[2,512,256]{2,1,0:T(8,128)}), f32[2,512,256]{2,1,0:T(8,128)}) %all-reduce.5.cloned.1.call-update) | async-done | bytes 1048592 | tf_op jit(solution)/shard_map/psum | solution.py:251
  234.7 29.4 %shard_map.57 = (bf16[32,512,256]{2,1,0:T(8,128)(2,1)}, f32[512,256]{1,0:T(8,128)}) custom-call(bf16[4,35,32,256]{3,2,1,0:T(8,128)(2,1)} %collective-permute-done.3.refs_0_, bf16[4,35,32,256]{3,2,1,0:T(8,128)(2,1)} %collective-permute-done.4.refs_1_, f32[1]{0:T(128)} %bitcast.16.refs_2_, s32[1]{0:T(128)} %bitcast.20.refs_3_, bf16[256,256]{1,0:T(8,128)(2,1)S(1)} %copy-done.4, ...), custom_call_target="tpu_custom_call" | custom-call | flops 3221225472 | bytes 31457280 | tf_op jit(solution)/shard_map/pallas_call | solution.py:234
  264.2 27.6 %shard_map.58.refs_5_ = f32[32,256,256]{2,1,0:T(8,128)} custom-call(bf16[4,35,32,256]{3,2,1,0:T(8,128)(2,1)S(1)} %all-to-all-done.refs_0_, bf16[4,35,32,256]{3,2,1,0:T(8,128)(2,1)} %copy-done.5, f32[1]{0:T(128)} %bitcast.16.refs_2_, s32[1]{0:T(128)} %bitcast.17.refs_3_, bf16[2,256,512]{2,1,0:T(8,128)(2,1)S(1)} %pad_maximum_fusion.5.refs_4_, ...), custom_call_target="tpu_custom_call" | custom-call | flops 3221225472 | bytes 37748736 | tf_op jit(solution)/shard_map/pallas_call | solution.py:275
  291.9 6.0 %all-reduce.7.cloned.1.call-done = f32[512,256]{1,0:T(8,128)} async-done(((f32[512,256]{1,0:T(8,128)}), f32[512,256]{1,0:T(8,128)}) %all-reduce.7.cloned.1.call-update) | async-done | bytes 524304 | tf_op jit(solution)/shard_map/psum | solution.py:254
  299.8 5.6 %shard_map.62 = bf16[4,8,64,256]{3,2,1,0:T(8,128)(2,1)S(1)} custom-call(bf16[4,35,32,256]{3,2,1,0:T(8,128)(2,1)S(1)} %all-to-all-done.refs_0_, bf16[4,35,32,256]{3,2,1,0:T(8,128)(2,1)} %copy-done.5, f32[1]{0:T(128)} %bitcast.16.refs_2_, s32[1]{0:T(128)} %bitcast.17.refs_3_, bf16[256,512]{1,0:T(8,128)(2,1)S(1)} %pad_maximum_fusion.6.refs_4_, ...), custom_call_target="tpu_custom_call" | custom-call | flops 268435456 | bytes 10485760 | tf_op jit(solution)/shard_map/pallas_call | solution.py:290
  306.4 4.3 %all-to-all-start.5 = ((bf16[4,8,64,256]{3,2,1,0:T(8,128)(2,1)}), bf16[4,8,64,256]{3,2,1,0:T(8,128)(2,1)}, u32[]{:S(2)}, u32[]{:S(2)}) async-start(bf16[4,8,64,256]{3,2,1,0:T(8,128)(2,1)} %copy-done.3), calls=%async_computation.5 | async-start | bytes 2097152 | tf_op jit(solution)/shard_map/all_to_all | solution.py:303
  310.6 5.6 %shard_map.61 = bf16[4,8,64,256]{3,2,1,0:T(8,128)(2,1)S(1)} custom-call(bf16[4,35,32,256]{3,2,1,0:T(8,128)(2,1)S(1)} %all-to-all-done.refs_0_, bf16[4,35,32,256]{3,2,1,0:T(8,128)(2,1)} %copy-done.5, f32[1]{0:T(128)} %bitcast.16.refs_2_, s32[1]{0:T(128)} %bitcast.17.refs_3_, bf16[256,512]{1,0:T(8,128)(2,1)S(1)} %pad_maximum_fusion.6.refs_4_, ...), custom_call_target="tpu_custom_call" | custom-call | flops 268435456 | bytes 10485760 | tf_op jit(solution)/shard_map/pallas_call | solution.py:290
  317.2 8.0 %all-to-all-done.5.refs_3_ = bf16[4,8,64,256]{3,2,1,0:T(8,128)(2,1)} async-done(((bf16[4,8,64,256]{3,2,1,0:T(8,128)(2,1)}), bf16[4,8,64,256]{3,2,1,0:T(8,128)(2,1)}, u32[]{:S(2)}, u32[]{:S(2)}) %all-to-all-start.5) | async-done | bytes 1048608 | tf_op jit(solution)/shard_map/all_to_all | solution.py:303
  329.4 5.5 %shard_map.59 = bf16[4,8,64,256]{3,2,1,0:T(8,128)(2,1)S(1)} custom-call(bf16[4,35,32,256]{3,2,1,0:T(8,128)(2,1)S(1)} %all-to-all-done.refs_0_, bf16[4,35,32,256]{3,2,1,0:T(8,128)(2,1)} %copy-done.5, f32[1]{0:T(128)} %bitcast.16.refs_2_, s32[1]{0:T(128)} %bitcast.17.refs_3_, bf16[256,512]{1,0:T(8,128)(2,1)S(1)} %pad_maximum_fusion.6.refs_4_, ...), custom_call_target="tpu_custom_call" | custom-call | flops 268435456 | bytes 10485760 | tf_op jit(solution)/shard_map/pallas_call | solution.py:290
  336.0 8.0 %all-to-all-done.4.refs_2_ = bf16[4,8,64,256]{3,2,1,0:T(8,128)(2,1)} async-done(((bf16[4,8,64,256]{3,2,1,0:T(8,128)(2,1)}), bf16[4,8,64,256]{3,2,1,0:T(8,128)(2,1)}, u32[]{:S(2)}, u32[]{:S(2)}) %all-to-all-start.4) | async-done | bytes 1048608 | tf_op jit(solution)/shard_map/all_to_all | solution.py:303
  344.0 4.3 %all-to-all-start.2 = ((bf16[4,8,64,256]{3,2,1,0:T(8,128)(2,1)}), bf16[4,8,64,256]{3,2,1,0:T(8,128)(2,1)}, u32[]{:S(2)}, u32[]{:S(2)}) async-start(bf16[4,8,64,256]{3,2,1,0:T(8,128)(2,1)} %copy-done), calls=%async_computation.2 | async-start | bytes 2097152 | tf_op jit(solution)/shard_map/all_to_all | solution.py:303
  348.2 5.6 %shard_map.60 = bf16[4,8,64,256]{3,2,1,0:T(8,128)(2,1)S(1)} custom-call(bf16[4,35,32,256]{3,2,1,0:T(8,128)(2,1)S(1)} %all-to-all-done.refs_0_, bf16[4,35,32,256]{3,2,1,0:T(8,128)(2,1)} %copy-done.5, f32[1]{0:T(128)} %bitcast.16.refs_2_, s32[1]{0:T(128)} %bitcast.17.refs_3_, bf16[256,512]{1,0:T(8,128)(2,1)S(1)} %pad_maximum_fusion.6.refs_4_, ...), custom_call_target="tpu_custom_call" | custom-call | flops 268435456 | bytes 10485760 | tf_op jit(solution)/shard_map/pallas_call | solution.py:290
  354.8 8.0 %all-to-all-done.2.refs_0_ = bf16[4,8,64,256]{3,2,1,0:T(8,128)(2,1)} async-done(((bf16[4,8,64,256]{3,2,1,0:T(8,128)(2,1)}), bf16[4,8,64,256]{3,2,1,0:T(8,128)(2,1)}, u32[]{:S(2)}, u32[]{:S(2)}) %all-to-all-start.2) | async-done | bytes 1048608 | tf_op jit(solution)/shard_map/all_to_all | solution.py:303
  362.7 17.9 %all_to_all.30.refs_1_ = bf16[4,8,64,256]{3,2,1,0:T(8,128)(2,1)S(1)} all-to-all(bf16[4,8,64,256]{3,2,1,0:T(8,128)(2,1)} %copy-done.1), channel_id=1, replica_groups=mesh['slab'=8,'orb'=4] {'orb'}, dimensions={0} | all-to-all | bytes 2097152 | tf_op jit(solution)/shard_map/all_to_all | solution.py:303
  380.7 6.9 %shard_map.63 = bf16[64,128,256]{2,1,0:T(8,128)(2,1)} custom-call(s32[64]{0:T(128)S(1)} %broadcast_subtract_fusion.offset_ref, bf16[4,8,64,256]{3,2,1,0:T(8,128)(2,1)} %all-to-all-done.2.refs_0_, bf16[4,8,64,256]{3,2,1,0:T(8,128)(2,1)S(1)} %all_to_all.30.refs_1_, bf16[4,8,64,256]{3,2,1,0:T(8,128)(2,1)} %all-to-all-done.4.refs_2_, ...), custom_call_target="tpu_custom_call" | custom-call | tf_op jit(solution)/shard_map/pallas_call | solution.py:306
  (65 shorter events, 48.1 us)
Async XLA Ops:
  24.4 4.4 %copy-start.7 = (f32[32,256]{1,0:T(8,128)S(1)}, f32[32,256]{1,0:T(8,128)}, u32[]{:S(2)}) copy-start(f32[32,256]{1,0:T(8,128)} %param.8) | copy-start | bytes 98308
  24.4 32.2 %all-to-all-start.1 = ((bf16[4,35,32,256]{3,2,1,0:T(8,128)(2,1)}), bf16[4,35,32,256]{3,2,1,0:T(8,128)(2,1)S(1)}, u32[]{:S(2)}, u32[]{:S(2)}) async-start(bf16[4,35,32,256]{3,2,1,0:T(8,128)(2,1)} %pad_maximum_fusion.3), calls=%async_computation.1 | async-start | bytes 4587520 | tf_op jit(solution)/shard_map/all_to_all | solution.py:203
  28.8 22.0 %collective-permute-start = (f32[32,256]{1,0:T(8,128)S(1)}, f32[32,256]{1,0:T(8,128)S(1)}, u32[]{:S(2)}, u32[]{:S(2)}) collective-permute-start(f32[32,256]{1,0:T(8,128)S(1)} %copy-done.7), channel_id=1, source_target_pairs={{0,28},{4,0},{8,4},{12,8},{16,12},{20,16},{24,20},{28,24},{1,29},{... | collective-permute-start | bytes 98312 | tf_op jit(solution)/shard_map/ppermute | solution.py:187
  50.8 40.9 %copy-start.4 = (bf16[256,256]{1,0:T(8,128)(2,1)S(1)}, bf16[256,256]{1,0:T(8,128)(2,1)}, u32[]{:S(2)}) copy-start(bf16[256,256]{1,0:T(8,128)(2,1)} %refs_4_.3) | copy-start | bytes 393220
  56.6 1.4 copy-start.5
  58.0 31.4 %all-to-all-start = ((bf16[4,35,32,256]{3,2,1,0:T(8,128)(2,1)}), bf16[4,35,32,256]{3,2,1,0:T(8,128)(2,1)S(1)}, u32[]{:S(2)}, u32[]{:S(2)}) async-start(bf16[4,35,32,256]{3,2,1,0:T(8,128)(2,1)} %pad_maximum_fusion.2), calls=%async_computation | async-start | bytes 4587520 | tf_op jit(solution)/shard_map/all_to_all | solution.py:203
  61.7 170.8 %all-reduce.5.cloned.1.call-start = ((), (), s32[]{:S(2)}) async-start(), calls=%async_computation.6 | async-start | bytes 2097152 | tf_op jit(solution)/shard_map/psum | solution.py:251
  61.7 54.6 %collective-permute-start.2 = (bf16[4,35,32,256]{3,2,1,0:T(8,128)(2,1)}, bf16[4,35,32,256]{3,2,1,0:T(8,128)(2,1)}, u32[]{:S(2)}, u32[]{:S(2)}) collective-permute-start(bf16[4,35,32,256]{3,2,1,0:T(8,128)(2,1)} %copy-done.5), channel_id=1, source_target_pairs={{0,4},{4,0},{8,12},{12,8},{16,20},{20,16},{24,28},{28,24},{1,5},{5... | collective-permute-start | bytes 6881288 | tf_op jit(solution)/shard_map/ppermute | solution.py:205
  89.4 74.5 %collective-permute-start.1 = (bf16[4,35,32,256]{3,2,1,0:T(8,128)(2,1)S(1)}, bf16[4,35,32,256]{3,2,1,0:T(8,128)(2,1)}, u32[]{:S(2)}, u32[]{:S(2)}) collective-permute-start(bf16[4,35,32,256]{3,2,1,0:T(8,128)(2,1)S(1)} %all-to-all-done.refs_0_), channel_id=1, source_target_pairs={{0,4},{4,0},{8,12},{12,8},{16,20},{20,16},{24,28},{28,24},{1,5},{5... | collective-permute-start | bytes 6881288 | tf_op jit(solution)/shard_map/ppermute | solution.py:205
  116.3 116.2 %collective-permute-start.4 = (bf16[4,35,32,256]{3,2,1,0:T(8,128)(2,1)}, bf16[4,35,32,256]{3,2,1,0:T(8,128)(2,1)}, u32[]{:S(2)}, u32[]{:S(2)}) collective-permute-start(bf16[4,35,32,256]{3,2,1,0:T(8,128)(2,1)} %collective-permute-done.2.refs_1_), channel_id=1, source_target_pairs={{0,8},{4,28},{8,16},{12,4},{16,24},{20,12},{24,0},{28,20},{1,9},{5... | collective-permute-start | bytes 6881288 | tf_op jit(solution)/shard_map/ppermute | solution.py:231
  163.9 68.5 %collective-permute-start.3 = (bf16[4,35,32,256]{3,2,1,0:T(8,128)(2,1)}, bf16[4,35,32,256]{3,2,1,0:T(8,128)(2,1)}, u32[]{:S(2)}, u32[]{:S(2)}) collective-permute-start(bf16[4,35,32,256]{3,2,1,0:T(8,128)(2,1)} %collective-permute-done.1.refs_0_), channel_id=1, source_target_pairs={{0,8},{4,28},{8,16},{12,4},{16,24},{20,12},{24,0},{28,20},{1,9},{5... | collective-permute-start | bytes 6881288 | tf_op jit(solution)/shard_map/ppermute | solution.py:231
  194.9 1.1 copy-start.6
  196.0 101.8 %all-reduce.7.cloned.1.call-start = ((), (), s32[]{:S(2)}) async-start(), calls=%async_computation.7 | async-start | bytes 1048576 | tf_op jit(solution)/shard_map/psum | solution.py:254
  305.4 1.0 copy-start.3
  306.4 18.8 %all-to-all-start.5 = ((bf16[4,8,64,256]{3,2,1,0:T(8,128)(2,1)}), bf16[4,8,64,256]{3,2,1,0:T(8,128)(2,1)}, u32[]{:S(2)}, u32[]{:S(2)}) async-start(bf16[4,8,64,256]{3,2,1,0:T(8,128)(2,1)} %copy-done.3), calls=%async_computation.5 | async-start | bytes 2097152 | tf_op jit(solution)/shard_map/all_to_all | solution.py:303
  316.2 1.0 copy-start.2
  325.2 18.8 %all-to-all-start.4 = ((bf16[4,8,64,256]{3,2,1,0:T(8,128)(2,1)}), bf16[4,8,64,256]{3,2,1,0:T(8,128)(2,1)}, u32[]{:S(2)}, u32[]{:S(2)}) async-start(bf16[4,8,64,256]{3,2,1,0:T(8,128)(2,1)} %copy-done.2), calls=%async_computation.4 | async-start | bytes 2097152 | tf_op jit(solution)/shard_map/all_to_all | solution.py:303
  335.0 1.0 copy-start
  344.0 18.8 %all-to-all-start.2 = ((bf16[4,8,64,256]{3,2,1,0:T(8,128)(2,1)}), bf16[4,8,64,256]{3,2,1,0:T(8,128)(2,1)}, u32[]{:S(2)}, u32[]{:S(2)}) async-start(bf16[4,8,64,256]{3,2,1,0:T(8,128)(2,1)} %copy-done), calls=%async_computation.2 | async-start | bytes 2097152 | tf_op jit(solution)/shard_map/all_to_all | solution.py:303
  353.8 1.0 copy-start.1
Sparse Core Ops, SparseCore 0:
  196.1 36.2 all-reduce.4
  264.3 33.5 all-reduce.6

commit v4 on v3

--- a/solution.py
+++ b/solution.py
@@ -247,8 +247,10 @@
             ),
         )(*parts, base, side.reshape(1), kin_cross, pots, right)
 
+    own_total = lax.psum(own_sums, "orb")
+    own_total, one_parts = lax.optimization_barrier((own_total, one_parts))
     one_left, one_sums = other(one_parts, first_side)
-    sums_a = lax.psum(jnp.stack([own_sums, one_sums]), "orb")
+    sums_a = lax.psum(one_sums, "orb")
     sums_a, two_parts = lax.optimization_barrier((sums_a, two_parts))
     two_left, two_sums = other(two_parts, 1 - first_side)
     sums_b = lax.psum(two_sums, "orb")
@@ -257,7 +259,7 @@
     mine = ids // BLOCK
     volume = 1.0 / (length * cross)
     weights = []
-    for group, sums in zip(groups, (sums_a[0], sums_a[1], sums_b)):
+    for group, sums in zip(groups, (own_total, sums_a, sums_b)):
         listed = lax.dynamic_slice_in_dim(pattern, group * blk_slab, blk_slab, 0)
         my_blocks = slab_id * blk_slab + mine
         kept = jnp.any(listed[:, :, None] == my_blocks[None, None, :], axis=1)

time: 398 us -> 427 us (1.073)
  waiting for transfers between devices: 143 us -> 173 us
    psum x1 -> x2, waiting for transfers between devices: 35.5 us -> 66.3 us  [the longest x1 33.2 us: per_device(): sums_a = lax.psum(one_sums, 'orb')]
    unnamed x20 -> x22, local copies, waits for them, and re-layouts: 9.29 us -> 9.3 us
  transfers between devices with their start and end apart: 12 -> 13, of which waited for: 8 -> 9; matrix products, arithmetic and copies ran while one was open for 5% -> 4% of each run, Pallas kernels for 25% -> 23%
where the time goes in v4:
time: 427 us; the launch traced here: 424 us
  waiting for transfers between devices  173 us (41%)
  Pallas kernels  140 us (33%)
  starting transfers between devices  34.5 us (8%)
  local copies, waits for them, and re-layouts  30.5 us (7%)
  blocking collectives  17.9 us (4%)
  other arithmetic  14.3 us (3%)
  between operations  13.4 us (3%)
    pallas_call x2, Pallas kernels, other(): pl.pallas_call(functools.partial(other_kernel, CHUNKS, length), grid=(nar...  58.9 us
    ppermute x2, waiting for transfers between devices, per_device(): one_parts.append(lax.ppermute(part, 'slab', swap))  45.8 us
    psum x1, waiting for transfers between devices, per_device(): sums_a = lax.psum(one_sums, 'orb')  33.2 us
    psum x1, waiting for transfers between devices, per_device(): own_total = lax.psum(own_sums, 'orb')  33 us
    all_to_all x2, waiting for transfers between devices, per_device(): lax.all_to_all(cut, 'orb', split_axis=0, concat_axis=0, tiled=True)  31.1 us
    pallas_call x1, Pallas kernels, per_device(): pl.pallas_call(functools.partial(near_kernel, CHUNKS), grid=(narrow,), in...  27.6 us
    pallas_call x1, Pallas kernels, per_device(): pl.pallas_call(functools.partial(own_kernel, CHUNKS, length), grid=(narro...  24.8 us
    all_to_all x3, waiting for transfers between devices, per_device(): lax.all_to_all(grad, 'orb', split_axis=0, concat_axis=0, tiled=True)  23.9 us
  transfers between devices with their start and end apart: 13, of which 9 were waited for; matrix products, arithmetic and copies ran while one was open for 4% of the time, Pallas kernels for 23%

profile of v4, /device:TPU:0, one launch (start us, length us, event | category | flops | bytes accessed | tf_op | source)
XLA Modules:
  0.0 423.7 jit_solution(8437959554136096075)
XLA Ops:
  15.9 6.3 %gather_fusion.1 = bf16[32,130,256]{2,0,1:T(8,128)(2,1)S(1)} fusion(bf16[32,258,256]{2,0,1:T(8,128)(2,1)} %pad_maximum_fusion.1, s32[32]{0:T(128)S(1)} %get-tuple-element.64), kind=kCustom, calls=%fused_computation.1 | custom fusion | bytes 4260224 | tf_op jit(solution)/shard_map/vmap()/gather | solution.py:163
  24.4 4.4 %all-to-all-start.1 = ((bf16[4,35,32,256]{3,2,1,0:T(8,128)(2,1)}), bf16[4,35,32,256]{3,2,1,0:T(8,128)(2,1)S(1)}, u32[]{:S(2)}, u32[]{:S(2)}) async-start(bf16[4,35,32,256]{3,2,1,0:T(8,128)(2,1)} %pad_maximum_fusion.3), calls=%async_computation.1 | async-start | bytes 4587520 | tf_op jit(solution)/shard_map/all_to_all | solution.py:203
  28.8 5.6 %collective-permute-start = (f32[32,256]{1,0:T(8,128)S(1)}, f32[32,256]{1,0:T(8,128)S(1)}, u32[]{:S(2)}, u32[]{:S(2)}) collective-permute-start(f32[32,256]{1,0:T(8,128)S(1)} %copy-done.8), channel_id=1, source_target_pairs={{0,28},{4,0},{8,4},{12,8},{16,12},{20,16},{24,20},{28,24},{1,29},{... | collective-permute-start | bytes 98312 | tf_op jit(solution)/shard_map/ppermute | solution.py:187
  39.5 7.6 %gather_fusion = bf16[32,130,256]{2,0,1:T(8,128)(2,1)} fusion(bf16[32,258,256]{2,0,1:T(8,128)(2,1)} %pad_maximum_fusion, s32[32]{0:T(128)S(1)} %get-tuple-element.65), kind=kCustom, calls=%fused_computation | custom fusion | bytes 4260224 | tf_op jit(solution)/shard_map/vmap()/gather | solution.py:163
  50.9 5.7 %all-to-all-done.1.refs_1_ = bf16[4,35,32,256]{3,2,1,0:T(8,128)(2,1)S(1)} async-done(((bf16[4,35,32,256]{3,2,1,0:T(8,128)(2,1)}), bf16[4,35,32,256]{3,2,1,0:T(8,128)(2,1)S(1)}, u32[]{:S(2)}, u32[]{:S(2)}) %all-to-all-start.1) | async-done | bytes 2293792 | tf_op jit(solution)/shard_map/all_to_all | solution.py:203
  64.1 25.3 %all-to-all-done.refs_0_ = bf16[4,35,32,256]{3,2,1,0:T(8,128)(2,1)S(1)} async-done(((bf16[4,35,32,256]{3,2,1,0:T(8,128)(2,1)}), bf16[4,35,32,256]{3,2,1,0:T(8,128)(2,1)S(1)}, u32[]{:S(2)}, u32[]{:S(2)}) %all-to-all-start) | async-done | bytes 2293792 | tf_op jit(solution)/shard_map/all_to_all | solution.py:203
  91.7 24.8 %shard_map.55 = (bf16[32,2,512,256]{3,2,1,0:T(8,128)(2,1)}, f32[512,256]{1,0:T(8,128)}) custom-call(bf16[4,35,32,256]{3,2,1,0:T(8,128)(2,1)S(1)} %all-to-all-done.refs_0_, bf16[4,35,32,256]{3,2,1,0:T(8,128)(2,1)} %copy-done.5, f32[1]{0:T(128)} %bitcast.16.refs_2_, bf16[256,256]{1,0:T(8,128)(2,1)S(1)} %copy-done.4, ...), custom_call_target="tpu_custom_call" | custom-call | flops 5368709120 | bytes 23068672 | tf_op jit(solution)/shard_map/pallas_call | solution.py:212
  118.1 45.8 %collective-permute-done.1.refs_0_ = bf16[4,35,32,256]{3,2,1,0:T(8,128)(2,1)} collective-permute-done((bf16[4,35,32,256]{3,2,1,0:T(8,128)(2,1)S(1)}, bf16[4,35,32,256]{3,2,1,0:T(8,128)(2,1)}, u32[]{:S(2)}, u32[]{:S(2)}) %collective-permute-start.1) | collective-permute-done | bytes 2293792 | tf_op jit(solution)/shard_map/ppermute | solution.py:205
  166.8 33.0 %all-reduce.6.cloned.1.call-done = f32[512,256]{1,0:T(8,128)} async-done(((f32[512,256]{1,0:T(8,128)}), f32[512,256]{1,0:T(8,128)}) %all-reduce.6.cloned.1.call-update) | async-done | bytes 524304 | tf_op jit(solution)/shard_map/psum | solution.py:250
  199.8 29.4 %shard_map.56 = (bf16[32,512,256]{2,1,0:T(8,128)(2,1)}, f32[512,256]{1,0:T(8,128)}) custom-call(bf16[4,35,32,256]{3,2,1,0:T(8,128)(2,1)} %collective-permute-done.1.refs_0_, bf16[4,35,32,256]{3,2,1,0:T(8,128)(2,1)} %collective-permute-done.2.refs_1_, f32[1]{0:T(128)} %bitcast.16.refs_2_, s32[1]{0:T(128)} %bitcast.17.refs_3_, bf16[256,256]{1,0:T(8,128)(2,1)S(1)} %copy-done.4, ...), custom_call_target="tpu_custom_call" | custom-call | flops 3221225472 | bytes 31457280 | tf_op jit(solution)/shard_map/pallas_call | solution.py:234
  229.5 33.2 %all-reduce.8.cloned.1.call-done = f32[512,256]{1,0:T(8,128)} async-done(((f32[512,256]{1,0:T(8,128)}), f32[512,256]{1,0:T(8,128)}) %all-reduce.8.cloned.1.call-update) | async-done | bytes 524304 | tf_op jit(solution)/shard_map/psum | solution.py:253
  264.7 29.4 %shard_map.57 = (bf16[32,512,256]{2,1,0:T(8,128)(2,1)}, f32[512,256]{1,0:T(8,128)}) custom-call(bf16[4,35,32,256]{3,2,1,0:T(8,128)(2,1)} %collective-permute-done.3.refs_0_, bf16[4,35,32,256]{3,2,1,0:T(8,128)(2,1)} %collective-permute-done.4.refs_1_, f32[1]{0:T(128)} %bitcast.16.refs_2_, s32[1]{0:T(128)} %bitcast.18.refs_3_, bf16[256,256]{1,0:T(8,128)(2,1)S(1)} %copy-done.4, ...), custom_call_target="tpu_custom_call" | custom-call | flops 3221225472 | bytes 31457280 | tf_op jit(solution)/shard_map/pallas_call | solution.py:234
  294.3 27.6 %shard_map.58.refs_5_ = f32[32,256,256]{2,1,0:T(8,128)} custom-call(bf16[4,35,32,256]{3,2,1,0:T(8,128)(2,1)S(1)} %all-to-all-done.refs_0_, bf16[4,35,32,256]{3,2,1,0:T(8,128)(2,1)} %copy-done.5, f32[1]{0:T(128)} %bitcast.16.refs_2_, s32[1]{0:T(128)} %bitcast.17.refs_3_, bf16[2,256,512]{2,1,0:T(8,128)(2,1)S(1)} %pad_maximum_fusion.4.refs_4_, ...), custom_call_target="tpu_custom_call" | custom-call | flops 3221225472 | bytes 37748736 | tf_op jit(solution)/shard_map/pallas_call | solution.py:277
  321.9 5.5 %all-reduce.10.cloned.1.call-done = f32[512,256]{1,0:T(8,128)} async-done(((f32[512,256]{1,0:T(8,128)}), f32[512,256]{1,0:T(8,128)}) %all-reduce.10.cloned.1.call-update) | async-done | bytes 524304 | tf_op jit(solution)/shard_map/psum | solution.py:256
  329.5 5.6 %shard_map.62 = bf16[4,8,64,256]{3,2,1,0:T(8,128)(2,1)S(1)} custom-call(bf16[4,35,32,256]{3,2,1,0:T(8,128)(2,1)S(1)} %all-to-all-done.refs_0_, bf16[4,35,32,256]{3,2,1,0:T(8,128)(2,1)} %copy-done.5, f32[1]{0:T(128)} %bitcast.16.refs_2_, s32[1]{0:T(128)} %bitcast.17.refs_3_, bf16[256,512]{1,0:T(8,128)(2,1)S(1)} %pad_maximum_fusion.5.refs_4_, ...), custom_call_target="tpu_custom_call" | custom-call | flops 268435456 | bytes 10485760 | tf_op jit(solution)/shard_map/pallas_call | solution.py:292
  336.0 4.3 %all-to-all-start.5 = ((bf16[4,8,64,256]{3,2,1,0:T(8,128)(2,1)}), bf16[4,8,64,256]{3,2,1,0:T(8,128)(2,1)}, u32[]{:S(2)}, u32[]{:S(2)}) async-start(bf16[4,8,64,256]{3,2,1,0:T(8,128)(2,1)} %copy-done.3), calls=%async_computation.5 | async-start | bytes 2097152 | tf_op jit(solution)/shard_map/all_to_all | solution.py:305
  340.3 5.6 %shard_map.61 = bf16[4,8,64,256]{3,2,1,0:T(8,128)(2,1)S(1)} custom-call(bf16[4,35,32,256]{3,2,1,0:T(8,128)(2,1)S(1)} %all-to-all-done.refs_0_, bf16[4,35,32,256]{3,2,1,0:T(8,128)(2,1)} %copy-done.5, f32[1]{0:T(128)} %bitcast.16.refs_2_, s32[1]{0:T(128)} %bitcast.17.refs_3_, bf16[256,512]{1,0:T(8,128)(2,1)S(1)} %pad_maximum_fusion.5.refs_4_, ...), custom_call_target="tpu_custom_call" | custom-call | flops 268435456 | bytes 10485760 | tf_op jit(solution)/shard_map/pallas_call | solution.py:292
  346.8 8.0 %all-to-all-done.5.refs_3_ = bf16[4,8,64,256]{3,2,1,0:T(8,128)(2,1)} async-done(((bf16[4,8,64,256]{3,2,1,0:T(8,128)(2,1)}), bf16[4,8,64,256]{3,2,1,0:T(8,128)(2,1)}, u32[]{:S(2)}, u32[]{:S(2)}) %all-to-all-start.5) | async-done | bytes 1048608 | tf_op jit(solution)/shard_map/all_to_all | solution.py:305
  359.1 5.5 %shard_map.59 = bf16[4,8,64,256]{3,2,1,0:T(8,128)(2,1)S(1)} custom-call(bf16[4,35,32,256]{3,2,1,0:T(8,128)(2,1)S(1)} %all-to-all-done.refs_0_, bf16[4,35,32,256]{3,2,1,0:T(8,128)(2,1)} %copy-done.5, f32[1]{0:T(128)} %bitcast.16.refs_2_, s32[1]{0:T(128)} %bitcast.17.refs_3_, bf16[256,512]{1,0:T(8,128)(2,1)S(1)} %pad_maximum_fusion.5.refs_4_, ...), custom_call_target="tpu_custom_call" | custom-call | flops 268435456 | bytes 10485760 | tf_op jit(solution)/shard_map/pallas_call | solution.py:292
  365.6 8.0 %all-to-all-done.4.refs_2_ = bf16[4,8,64,256]{3,2,1,0:T(8,128)(2,1)} async-done(((bf16[4,8,64,256]{3,2,1,0:T(8,128)(2,1)}), bf16[4,8,64,256]{3,2,1,0:T(8,128)(2,1)}, u32[]{:S(2)}, u32[]{:S(2)}) %all-to-all-start.4) | async-done | bytes 1048608 | tf_op jit(solution)/shard_map/all_to_all | solution.py:305
  377.8 5.6 %shard_map.60 = bf16[4,8,64,256]{3,2,1,0:T(8,128)(2,1)S(1)} custom-call(bf16[4,35,32,256]{3,2,1,0:T(8,128)(2,1)S(1)} %all-to-all-done.refs_0_, bf16[4,35,32,256]{3,2,1,0:T(8,128)(2,1)} %copy-done.5, f32[1]{0:T(128)} %bitcast.16.refs_2_, s32[1]{0:T(128)} %bitcast.17.refs_3_, bf16[256,512]{1,0:T(8,128)(2,1)S(1)} %pad_maximum_fusion.5.refs_4_, ...), custom_call_target="tpu_custom_call" | custom-call | flops 268435456 | bytes 10485760 | tf_op jit(solution)/shard_map/pallas_call | solution.py:292
  384.4 8.0 %all-to-all-done.2.refs_0_ = bf16[4,8,64,256]{3,2,1,0:T(8,128)(2,1)} async-done(((bf16[4,8,64,256]{3,2,1,0:T(8,128)(2,1)}), bf16[4,8,64,256]{3,2,1,0:T(8,128)(2,1)}, u32[]{:S(2)}, u32[]{:S(2)}) %all-to-all-start.2) | async-done | bytes 1048608 | tf_op jit(solution)/shard_map/all_to_all | solution.py:305
  392.3 17.9 %all_to_all.30.refs_1_ = bf16[4,8,64,256]{3,2,1,0:T(8,128)(2,1)S(1)} all-to-all(bf16[4,8,64,256]{3,2,1,0:T(8,128)(2,1)} %copy-done.1), channel_id=1, replica_groups=mesh['slab'=8,'orb'=4] {'orb'}, dimensions={0} | all-to-all | bytes 2097152 | tf_op jit(solution)/shard_map/all_to_all | solution.py:305
  410.3 6.9 %shard_map.63 = bf16[64,128,256]{2,1,0:T(8,128)(2,1)} custom-call(s32[64]{0:T(128)S(1)} %broadcast_subtract_fusion.offset_ref, bf16[4,8,64,256]{3,2,1,0:T(8,128)(2,1)} %all-to-all-done.2.refs_0_, bf16[4,8,64,256]{3,2,1,0:T(8,128)(2,1)S(1)} %all_to_all.30.refs_1_, bf16[4,8,64,256]{3,2,1,0:T(8,128)(2,1)} %all-to-all-done.4.refs_2_, ...), custom_call_target="tpu_custom_call" | custom-call | tf_op jit(solution)/shard_map/pallas_call | solution.py:308
  (71 shorter events, 51.2 us)
Async XLA Ops:
  24.4 4.4 %copy-start.8 = (f32[32,256]{1,0:T(8,128)S(1)}, f32[32,256]{1,0:T(8,128)}, u32[]{:S(2)}) copy-start(f32[32,256]{1,0:T(8,128)} %param.8) | copy-start | bytes 98308
  24.4 32.2 %all-to-all-start.1 = ((bf16[4,35,32,256]{3,2,1,0:T(8,128)(2,1)}), bf16[4,35,32,256]{3,2,1,0:T(8,128)(2,1)S(1)}, u32[]{:S(2)}, u32[]{:S(2)}) async-start(bf16[4,35,32,256]{3,2,1,0:T(8,128)(2,1)} %pad_maximum_fusion.3), calls=%async_computation.1 | async-start | bytes 4587520 | tf_op jit(solution)/shard_map/all_to_all | solution.py:203
  28.8 22.0 %collective-permute-start = (f32[32,256]{1,0:T(8,128)S(1)}, f32[32,256]{1,0:T(8,128)S(1)}, u32[]{:S(2)}, u32[]{:S(2)}) collective-permute-start(f32[32,256]{1,0:T(8,128)S(1)} %copy-done.8), channel_id=1, source_target_pairs={{0,28},{4,0},{8,4},{12,8},{16,12},{20,16},{24,20},{28,24},{1,29},{... | collective-permute-start | bytes 98312 | tf_op jit(solution)/shard_map/ppermute | solution.py:187
  50.8 40.9 %copy-start.4 = (bf16[256,256]{1,0:T(8,128)(2,1)S(1)}, bf16[256,256]{1,0:T(8,128)(2,1)}, u32[]{:S(2)}) copy-start(bf16[256,256]{1,0:T(8,128)(2,1)} %refs_4_.3) | copy-start | bytes 393220
  56.6 1.4 copy-start.5
  58.0 31.4 %all-to-all-start = ((bf16[4,35,32,256]{3,2,1,0:T(8,128)(2,1)}), bf16[4,35,32,256]{3,2,1,0:T(8,128)(2,1)S(1)}, u32[]{:S(2)}, u32[]{:S(2)}) async-start(bf16[4,35,32,256]{3,2,1,0:T(8,128)(2,1)} %pad_maximum_fusion.2), calls=%async_computation | async-start | bytes 4587520 | tf_op jit(solution)/shard_map/all_to_all | solution.py:203
  61.7 138.2 %all-reduce.6.cloned.1.call-start = ((), (), s32[]{:S(2)}) async-start(), calls=%async_computation.6 | async-start | bytes 1048576 | tf_op jit(solution)/shard_map/psum | solution.py:250
  61.7 54.8 %collective-permute-start.2 = (bf16[4,35,32,256]{3,2,1,0:T(8,128)(2,1)}, bf16[4,35,32,256]{3,2,1,0:T(8,128)(2,1)}, u32[]{:S(2)}, u32[]{:S(2)}) collective-permute-start(bf16[4,35,32,256]{3,2,1,0:T(8,128)(2,1)} %copy-done.5), channel_id=1, source_target_pairs={{0,4},{4,0},{8,12},{12,8},{16,20},{20,16},{24,28},{28,24},{1,5},{5... | collective-permute-start | bytes 6881288 | tf_op jit(solution)/shard_map/ppermute | solution.py:205
  89.4 74.5 %collective-permute-start.1 = (bf16[4,35,32,256]{3,2,1,0:T(8,128)(2,1)S(1)}, bf16[4,35,32,256]{3,2,1,0:T(8,128)(2,1)}, u32[]{:S(2)}, u32[]{:S(2)}) collective-permute-start(bf16[4,35,32,256]{3,2,1,0:T(8,128)(2,1)S(1)} %all-to-all-done.refs_0_), channel_id=1, source_target_pairs={{0,4},{4,0},{8,12},{12,8},{16,20},{20,16},{24,28},{28,24},{1,5},{5... | collective-permute-start | bytes 6881288 | tf_op jit(solution)/shard_map/ppermute | solution.py:205
  91.7 74.1 %copy-start.7 = (s32[32,5]{0,1:T(8,128)S(1)}, s32[32,5]{0,1:T(8,128)}, u32[]{:S(2)}) copy-start(s32[32,5]{0,1:T(8,128)} %param.9) | copy-start | bytes 1924
  116.5 146.2 %collective-permute-start.4 = (bf16[4,35,32,256]{3,2,1,0:T(8,128)(2,1)}, bf16[4,35,32,256]{3,2,1,0:T(8,128)(2,1)}, u32[]{:S(2)}, u32[]{:S(2)}) collective-permute-start(bf16[4,35,32,256]{3,2,1,0:T(8,128)(2,1)} %collective-permute-done.2.refs_1_), channel_id=1, source_target_pairs={{0,8},{4,28},{8,16},{12,4},{16,24},{20,12},{24,0},{28,20},{1,9},{5... | collective-permute-start | bytes 6881288 | tf_op jit(solution)/shard_map/ppermute | solution.py:231
  163.9 98.8 %collective-permute-start.3 = (bf16[4,35,32,256]{3,2,1,0:T(8,128)(2,1)}, bf16[4,35,32,256]{3,2,1,0:T(8,128)(2,1)}, u32[]{:S(2)}, u32[]{:S(2)}) collective-permute-start(bf16[4,35,32,256]{3,2,1,0:T(8,128)(2,1)} %collective-permute-done.1.refs_0_), channel_id=1, source_target_pairs={{0,8},{4,28},{8,16},{12,4},{16,24},{20,12},{24,0},{28,20},{1,9},{5... | collective-permute-start | bytes 6881288 | tf_op jit(solution)/shard_map/ppermute | solution.py:231
  166.0 96.7 %all-reduce.8.cloned.1.call-start = ((), (), s32[]{:S(2)}) async-start(), calls=%async_computation.7 | async-start | bytes 1048576 | tf_op jit(solution)/shard_map/psum | solution.py:253
  199.8 29.5 %copy-start.6 = (f32[512,256]{1,0:T(8,128)S(1)}, f32[512,256]{1,0:T(8,128)}, u32[]{:S(2)}) copy-start(f32[512,256]{1,0:T(8,128)} %all-reduce.6.cloned.1.call-done) | copy-start | bytes 1572868
  229.3 98.1 %all-reduce.10.cloned.1.call-start = ((), (), s32[]{:S(2)}) async-start(), calls=%async_computation.8 | async-start | bytes 1048576 | tf_op jit(solution)/shard_map/psum | solution.py:256
  335.0 1.0 copy-start.3
  336.0 18.8 %all-to-all-start.5 = ((bf16[4,8,64,256]{3,2,1,0:T(8,128)(2,1)}), bf16[4,8,64,256]{3,2,1,0:T(8,128)(2,1)}, u32[]{:S(2)}, u32[]{:S(2)}) async-start(bf16[4,8,64,256]{3,2,1,0:T(8,128)(2,1)} %copy-done.3), calls=%async_computation.5 | async-start | bytes 2097152 | tf_op jit(solution)/shard_map/all_to_all | solution.py:305
  345.9 1.0 copy-start.2
  354.8 18.8 %all-to-all-start.4 = ((bf16[4,8,64,256]{3,2,1,0:T(8,128)(2,1)}), bf16[4,8,64,256]{3,2,1,0:T(8,128)(2,1)}, u32[]{:S(2)}, u32[]{:S(2)}) async-start(bf16[4,8,64,256]{3,2,1,0:T(8,128)(2,1)} %copy-done.2), calls=%async_computation.4 | async-start | bytes 2097152 | tf_op jit(solution)/shard_map/all_to_all | solution.py:305
  364.6 1.0 copy-start
  373.6 18.8 %all-to-all-start.2 = ((bf16[4,8,64,256]{3,2,1,0:T(8,128)(2,1)}), bf16[4,8,64,256]{3,2,1,0:T(8,128)(2,1)}, u32[]{:S(2)}, u32[]{:S(2)}) async-start(bf16[4,8,64,256]{3,2,1,0:T(8,128)(2,1)} %copy-done), calls=%async_computation.2 | async-start | bytes 2097152 | tf_op jit(solution)/shard_map/all_to_all | solution.py:305
  383.4 1.0 copy-start.1
Sparse Core Ops, SparseCore 0:
  166.1 33.7 all-reduce.5
  229.4 33.2 all-reduce.7
  294.3 33.0 all-reduce.9
